TPU v7x, 32 devices: a whole 2x2x4 slice. The times are simulated.
32 devices in a mesh: fsdp: 16 (over z, x, core), tp: 2 (over y).
Axes of the slice: x: 2, y: 2, z: 4, core: 2. Of those that a mesh axis runs over, the one named last changes fastest.
Arguments:
- tokens: bfloat16 [8192, 768], P(('fsdp', 'tp')), may hold values from -6 to 6
- lengths: int32 [16], replicated, may hold values from 288 to 512, as said below
- routes: int32 [8192, 1], P('fsdp'), may hold values from 0 to 3; in each aligned block of 512 rows (0 to 511, 512 to 1023, ...) at most 192 rows name the same one
- cotangent: bfloat16 [8192, 768], P(('fsdp', 'tp')), may hold values from -6 to 6
- gain_attn: bfloat16 [768], replicated, may hold values from 0.5 to 1.5
- gain_moe: bfloat16 [768], replicated, may hold values from 0.5 to 1.5
- qkv_weight: bfloat16 [768, 3, 768], P('fsdp', None, 'tp'), may hold values from -0.21875 to 0.21875
- out_weight: bfloat16 [768, 768], P('fsdp', 'tp'), may hold values from -1.75 to 1.75
- rel_table: bfloat16 [32, 12], replicated, may hold values from -4 to 4
- router_weight: bfloat16 [768, 4], replicated, may hold values from -0.15625 to 0.15625
- w_in: bfloat16 [768, 4, 3072], P('fsdp', None, 'tp'), may hold values from -0.21875 to 0.21875
- w_out: bfloat16 [768, 4, 3072], P('fsdp', None, 'tp'), may hold values from -0.625 to 0.625
Outputs:
- mixed: bfloat16 [8192, 768], P(('fsdp', 'tp'))
- balance: float32 [], replicated
- grad_tokens: bfloat16 [8192, 768], P(('fsdp', 'tp'))
- grad_gain_attn: float32 [768], replicated
- grad_gain_moe: float32 [768], replicated
- grad_qkv: float32 [768, 3, 768], P('fsdp', None, 'tp')
- grad_out: float32 [768, 768], P('fsdp', 'tp')
- grad_table: float32 [32, 12], replicated
- grad_router: float32 [768, 4], replicated
- grad_in: float32 [768, 4, 3072], P('fsdp', None, 'tp')
- grad_down: float32 [768, 4, 3072], P('fsdp', None, 'tp')
Inputs may be any that keep to these rules, and one draw needn't show every extreme that they name: `lengths`: some sequence has exactly 512 real tokens. `routes`: in each aligned block of 512 rows (one sequence) no expert is named by more than 192 rows, a bound that some block reaches.
All inputs are finite; a program needn't handle non-finite values.
Results may differ from a plain program's by a relative error of at most 0.017.
Values may be sent and summed in bfloat16 or wider, within the bound.
A program may use at most 192 MiB of HBM per device.

v0:
```python
import math

import jax
import jax.numpy as jnp
from jax import lax
from jax.sharding import PartitionSpec as P

HEADS = 12
HD = 64
BUCKETS = 32
EXP = 4


epsilon = 1e-06
balance_weight = 0.01
far_edges = (12, 16, 23, 32, 46, 64, 91)
highest = lax.Precision.HIGHEST


def bucket_index(query_pos, key_pos):
    offset = key_pos[None, :] - query_pos[:, None]
    spread = jnp.abs(offset)
    far_bucket = 8 + sum(((spread >= edge).astype(jnp.int32) for edge in far_edges))
    near_bucket = jnp.where(spread < 8, spread, far_bucket)
    return near_bucket + jnp.where(offset > 0, 16, 0).astype(jnp.int32)


def norm_rows(values, gain_vec):
    factor = lax.rsqrt(jnp.mean(values * values, axis=-1, keepdims=True) + epsilon)
    hat_rows = values * factor
    return (hat_rows, factor, (hat_rows * gain_vec).astype(jnp.bfloat16))


def norm_back(grad_normed, hat_rows, factor, gain_vec):
    grad_hat = grad_normed * gain_vec
    inner = jnp.mean(grad_hat * hat_rows, axis=-1, keepdims=True)
    return (factor * (grad_hat - hat_rows * inner), jnp.sum(grad_normed * hat_rows, axis=0))


def split_heads(row_block, heads_local):
    return row_block.reshape(row_block.shape[0], heads_local, HD).transpose(1, 0, 2)


def join_heads(head_block):
    return head_block.transpose(1, 0, 2).reshape(
        head_block.shape[1], head_block.shape[0] * head_block.shape[2]
    )


def per_device(
    tokens,
    lengths,
    routes,
    cotangent,
    gain_attn,
    gain_moe,
    qkv_weight,
    out_weight,
    rel_table,
    router_weight,
    w_in,
    w_out,
):
    tok_dev, model_width = tokens.shape
    tp_count = lax.axis_size("tp")
    seq_len = tok_dev * tp_count
    capacity = 3 * seq_len // 8
    slot_count = EXP * capacity
    heads_local = HEADS // tp_count
    hidden_local = w_in.shape[2]
    head_width = qkv_weight.shape[2]
    shard_rows = qkv_weight.shape[0]
    tp_index = lax.axis_index("tp")
    group_id = lax.axis_index("fsdp")
    length = lax.dynamic_index_in_dim(lengths, group_id, 0, keepdims=False)
    all_pos = jnp.arange(seq_len, dtype=jnp.int32)
    key_valid = all_pos < length
    local_pos = tp_index * tok_dev + jnp.arange(tok_dev, dtype=jnp.int32)
    local_valid = (local_pos < length).astype(jnp.float32)[:, None]
    score_scale = 1.0 / math.sqrt(HD)
    block_rows = min(512, seq_len)
    bucket_ids = jnp.arange(BUCKETS, dtype=jnp.int32)
    qkv_full, out_full, in_full, down_full = (
        lax.all_gather(qkv_weight, "fsdp", axis=0, tiled=True),
        lax.all_gather(out_weight, "fsdp", axis=0, tiled=True),
        lax.all_gather(w_in, "fsdp", axis=0, tiled=True),
        lax.all_gather(w_out, "fsdp", axis=0, tiled=True),
    )
    token_f = tokens.astype(jnp.float32)
    gain_one = gain_attn.astype(jnp.float32)
    gain_two = gain_moe.astype(jnp.float32)
    hat_attn, factor_attn, normed_attn = norm_rows(token_f, gain_one)
    attn_in = lax.all_gather(normed_attn, "tp", axis=0, tiled=True)
    qkv = jnp.einsum("sd,dch->csh", attn_in, qkv_full, preferred_element_type=jnp.float32).astype(
        jnp.bfloat16
    )
    query_heads = split_heads(qkv[0], heads_local)
    key_heads = split_heads(qkv[1], heads_local)
    value_heads = split_heads(qkv[2], heads_local)
    table_local = lax.dynamic_slice_in_dim(rel_table, tp_index * heads_local, heads_local, 1)

    def bucket_table(row_start):
        buckets = bucket_index(row_start + jnp.arange(block_rows, dtype=jnp.int32), all_pos)
        return (buckets[:, :, None] == bucket_ids[None, None, :]).astype(jnp.bfloat16)

    def scores_for(bias_block):
        raw_scores = (
            jnp.einsum("hqe,hke->hqk", query_heads, key_heads, preferred_element_type=jnp.float32)
            * score_scale
            + bias_block
        )
        return (jnp.where(key_valid[None, None, :], raw_scores, -jnp.inf), query_heads)

    block_id = 0
    bucket_onehot = bucket_table(block_id * block_rows)
    bias_block = jnp.einsum(
        "qkb,bh->hqk", bucket_onehot, table_local, preferred_element_type=jnp.float32
    )
    biases = [bias_block]
    masked, _ = scores_for(bias_block)
    row_max = jnp.max(masked, axis=-1, keepdims=True)
    exp_scores = jnp.exp(masked - row_max)
    row_total = jnp.sum(exp_scores, axis=-1, keepdims=True)
    attn_probs = exp_scores / row_total
    context = jnp.einsum(
        "hqk,hke->hqe",
        attn_probs.astype(jnp.bfloat16),
        value_heads,
        preferred_element_type=jnp.float32,
    )
    contexts = context.astype(jnp.bfloat16)
    log_sums = [row_max + jnp.log(row_total)]
    context_flat = join_heads(contexts)
    attn_sum = lax.psum_scatter(
        lax.dot_general(
            context_flat, out_full, (((1,), (1,)), ((), ())), preferred_element_type=jnp.float32
        ),
        "tp",
        scatter_dimension=0,
        tiled=True,
    )
    mid = token_f + attn_sum * local_valid
    hat_moe, factor_moe, normed_moe = norm_rows(mid, gain_two)
    router_f = router_weight.astype(jnp.float32)
    logits = jnp.dot(normed_moe, router_weight, preferred_element_type=jnp.float32)
    router_probs = jax.nn.softmax(logits, axis=-1)
    routes_group = routes[:, 0]
    route_local = lax.dynamic_slice_in_dim(routes_group, tp_index * tok_dev, tok_dev)
    expert_ids = jnp.arange(EXP, dtype=jnp.int32)
    onehot_local = (route_local[:, None] == expert_ids[None, :]).astype(jnp.float32)
    gate = jnp.sum(router_probs * onehot_local, axis=1, keepdims=True)
    counts_local = jnp.sum(onehot_local * local_valid, axis=0)
    prob_local = jnp.sum(local_valid * router_probs, axis=0)
    counts_all, prob_all = lax.psum((counts_local, prob_local), ("fsdp", "tp"))
    total_tokens = jnp.sum(lengths).astype(jnp.float32)
    fraction = counts_all / total_tokens
    balance = EXP * jnp.sum(fraction * (prob_all / total_tokens))
    moe_in = lax.all_gather(normed_moe, "tp", axis=0, tiled=True)
    chosen = (routes_group[:, None] == expert_ids[None, :]).astype(jnp.int32) * key_valid.astype(
        jnp.int32
    )[:, None]
    slot_ids = jnp.sum(chosen * (jnp.cumsum(chosen, axis=0) - 1), axis=1)
    flat_index = jnp.where(key_valid, routes_group * capacity + slot_ids, slot_count)
    owner = jnp.zeros((slot_count + 1,), jnp.int32).at[flat_index].set(all_pos)[:slot_count]
    filled = (jnp.zeros((slot_count + 1,), jnp.int32).at[flat_index].set(1)[:slot_count] > 0)[
        :, None
    ]
    zero_bf = jnp.zeros((), jnp.bfloat16)
    dispatched = jnp.where(filled, moe_in[owner], zero_bf).reshape(EXP, capacity, model_width)
    pre_act = jnp.einsum("ecd,def->ecf", dispatched, in_full, preferred_element_type=jnp.float32)
    act = jax.nn.gelu(pre_act, approximate=False).astype(jnp.bfloat16)
    expert_part = jnp.einsum("ecf,def->ecd", act, down_full, preferred_element_type=jnp.float32)
    padded_part = jnp.concatenate(
        [expert_part.reshape(slot_count, model_width), jnp.zeros((1, model_width), jnp.float32)],
        axis=0,
    )
    combined = lax.psum_scatter(
        padded_part[flat_index].astype(jnp.bfloat16), "tp", scatter_dimension=0, tiled=True
    ).astype(jnp.float32)
    mixed = (mid + gate * combined * local_valid).astype(jnp.bfloat16)
    qkv_back, out_back, in_back, down_back = (
        lax.all_gather(qkv_weight, "fsdp", axis=0, tiled=True),
        lax.all_gather(out_weight, "fsdp", axis=0, tiled=True),
        lax.all_gather(w_in, "fsdp", axis=0, tiled=True),
        lax.all_gather(w_out, "fsdp", axis=0, tiled=True),
    )
    grad_out = cotangent.astype(jnp.float32)
    grad_gate = jnp.sum(grad_out * combined * local_valid, axis=1, keepdims=True)
    scaled_grad = (grad_out * gate * local_valid).astype(jnp.bfloat16)
    grad_rows = lax.all_gather(scaled_grad, "tp", axis=0, tiled=True)
    grad_expert = jnp.where(filled, grad_rows[owner], zero_bf).reshape(EXP, capacity, model_width)
    grad_act = jnp.einsum(
        "ecd,def->ecf", grad_expert, down_back, preferred_element_type=jnp.float32
    )
    _, gelu_pull = jax.vjp(lambda inner_value: jax.nn.gelu(inner_value, approximate=False), pre_act)
    grad_pre = gelu_pull(grad_act)[0].astype(jnp.bfloat16)
    grad_dispatch = jnp.einsum(
        "ecf,def->ecd", grad_pre, in_back, preferred_element_type=jnp.float32
    )
    padded_dispatch = jnp.concatenate(
        [grad_dispatch.reshape(slot_count, model_width), jnp.zeros((1, model_width), jnp.float32)],
        axis=0,
    )
    grad_normed = lax.psum_scatter(
        padded_dispatch[flat_index], "tp", scatter_dimension=0, tiled=True
    )
    aux_grad = balance_weight * EXP * fraction / total_tokens
    grad_probs = onehot_local * grad_gate + local_valid * aux_grad[None, :]
    grad_logits = router_probs * (
        grad_probs - jnp.sum(router_probs * grad_probs, axis=1, keepdims=True)
    )
    grad_router = jnp.einsum(
        "sd,se->de", normed_moe.astype(jnp.float32), grad_logits, precision=highest
    )
    grad_normed = grad_normed + jnp.einsum("se,de->sd", grad_logits, router_f, precision=highest)
    grad_mid_norm, grad_gain_moe = norm_back(grad_normed, hat_moe, factor_moe, gain_two)
    grad_mid = grad_out + grad_mid_norm
    grad_branch = (grad_mid * local_valid).astype(jnp.bfloat16)
    grad_branch_all = lax.all_gather(grad_branch, "tp", axis=0, tiled=True)
    grad_context = jnp.dot(grad_branch_all, out_back, preferred_element_type=jnp.float32).astype(
        jnp.bfloat16
    )
    grad_context_heads = split_heads(grad_context, heads_local)
    block_id = 0
    row_start = block_id * block_rows
    masked, query_block = scores_for(biases[block_id])
    attn_probs = jnp.exp(masked - log_sums[block_id])
    grad_value = jnp.einsum(
        "hqk,hqe->hke",
        attn_probs.astype(jnp.bfloat16),
        grad_context_heads,
        preferred_element_type=jnp.float32,
    )
    grad_p = jnp.einsum(
        "hqe,hke->hqk", grad_context_heads, value_heads, preferred_element_type=jnp.float32
    )
    grad_scores = (
        attn_probs * (grad_p - jnp.sum(attn_probs * grad_p, axis=-1, keepdims=True))
    ).astype(jnp.bfloat16)
    query_grads = (
        jnp.einsum("hqk,hke->hqe", grad_scores, key_heads, preferred_element_type=jnp.float32)
        * score_scale
    )
    grad_key = (
        jnp.einsum("hqk,hqe->hke", grad_scores, query_block, preferred_element_type=jnp.float32)
        * score_scale
    )
    bucket_onehot = bucket_table(row_start)
    grad_table_local = jnp.einsum(
        "hqk,qkb->hb", grad_scores, bucket_onehot, preferred_element_type=jnp.float32
    )
    grad_qkv_rows = jnp.stack(
        [
            join_heads(query_grads.astype(jnp.bfloat16)),
            join_heads(grad_key.astype(jnp.bfloat16)),
            join_heads(grad_value.astype(jnp.bfloat16)),
        ]
    )
    grad_attn_part = jnp.einsum(
        "csh,dch->sd", grad_qkv_rows, qkv_back, preferred_element_type=jnp.float32
    )
    grad_attn_in = lax.psum_scatter(
        grad_attn_part.astype(jnp.bfloat16), "tp", scatter_dimension=0, tiled=True
    ).astype(jnp.float32)
    grad_token_norm, grad_gain_attn = norm_back(grad_attn_in, hat_attn, factor_attn, gain_one)
    grad_tokens = (grad_mid + grad_token_norm).astype(jnp.bfloat16)
    table_full = lax.dynamic_update_slice(
        jnp.zeros((BUCKETS, HEADS), jnp.float32), grad_table_local.T, (0, tp_index * heads_local)
    )
    in_term = jnp.einsum("ecd,ecf->def", dispatched, grad_pre, preferred_element_type=jnp.float32)
    down_term = jnp.einsum("ecd,ecf->def", grad_expert, act, preferred_element_type=jnp.float32)
    qkv_term = jnp.einsum("sd,csh->dch", attn_in, grad_qkv_rows, preferred_element_type=jnp.float32)
    out_term = jnp.einsum(
        "sj,si->ji", grad_branch_all, context_flat, preferred_element_type=jnp.float32
    )
    summed_all = lax.psum_scatter(
        jnp.concatenate(
            [
                jnp.concatenate(
                    [
                        qkv_term.reshape(shard_rows * lax.axis_size("fsdp"), 3 * head_width),
                        out_term,
                    ],
                    axis=1,
                ),
                jnp.concatenate(
                    [
                        in_term.reshape(shard_rows * lax.axis_size("fsdp"), EXP * hidden_local),
                        down_term.reshape(shard_rows * lax.axis_size("fsdp"), EXP * hidden_local),
                    ],
                    axis=1,
                ),
            ],
            axis=1,
        ),
        "fsdp",
        scatter_dimension=0,
        tiled=True,
    )
    summed = summed_all[:, : 4 * head_width]
    grad_qkv = summed[:, : 3 * head_width].reshape(shard_rows, 3, head_width)
    grad_out_shard = summed[:, 3 * head_width : 4 * head_width]
    summed = summed_all[:, 4 * head_width :]
    grad_in_part = summed[:, : EXP * hidden_local].reshape(shard_rows, EXP, hidden_local)
    grad_down_part = summed[:, EXP * hidden_local :].reshape(shard_rows, EXP, hidden_local)
    gain_attn_sum, gain_moe_sum, router_sum, table_sum = lax.psum(
        (grad_gain_attn, grad_gain_moe, grad_router, table_full), ("fsdp", "tp")
    )
    return (
        mixed,
        balance,
        grad_tokens,
        gain_attn_sum,
        gain_moe_sum,
        grad_qkv,
        grad_out_shard,
        table_sum,
        router_sum,
        grad_in_part,
        grad_down_part,
    )


def solution(mesh):
    placed = (
        P(("fsdp", "tp"), None),
        P(),
        P("fsdp", None),
        P(("fsdp", "tp"), None),
        P(),
        P(),
        P("fsdp", None, "tp"),
        P("fsdp", "tp"),
        P(),
        P(),
        P("fsdp", None, "tp"),
        P("fsdp", None, "tp"),
    )
    return jax.shard_map(
        per_device,
        mesh=mesh,
        in_specs=placed,
        out_specs=(
            P(("fsdp", "tp"), None),
            P(),
            P(("fsdp", "tp"), None),
            P(),
            P(),
            P("fsdp", None, "tp"),
            P("fsdp", "tp"),
            P(),
            P(),
            P("fsdp", None, "tp"),
            P("fsdp", None, "tp"),
        ),
        check_vma=False,
    )
```

profile of v0, /device:TPU:0, one launch (start us, length us, event | category | flops | bytes accessed | tf_op | source)
XLA Modules:
  0.0 958.2 jit_solution(10933961103719061248)
XLA Ops:
  9.1 8.6 iota_compare_fusion
  17.7 46.2 %copy.40 = pred[512,512,32]{1,2,0:T(32,128)(4,1)} copy(pred[512,512,32]{0,2,1:T(32,128)(4,1)} %iota_compare_fusion) | data formatting | bytes 16777216 | tf_op jit(solution)/shard_map/eq | solution.py:104
  64.0 10.5 %fusion.71 = f32[6,512,512]{2,0,1:T(8,128)} fusion(pred[512,512,32]{1,2,0:T(32,128)(4,1)} %copy.40, bf16[32,12]{0,1:T(8,128)(2,1)S(1)} %copy-done.49, s32[]{:T(128)S(6)} %select_n.64), kind=kOutput, calls=%fused_computation.140 | convolution fusion | flops 100663296 | bytes 14682116 | tf_op jit(solution)/shard_map/qkb,bh->hqk/dot_general | solution.py:116
  74.5 9.2 copy.41
  85.7 12.8 %all_gather.28 = bf16[512,768]{1,0:T(8,128)(2,1)S(1)} all-gather(bf16[256,768]{1,0:T(8,128)(2,1)S(1)} %fusion.51), channel_id=1, replica_groups=mesh['fsdp'=16,'tp'=2] {'tp'}, dimensions={0}, use_global_device_ids=true | all-gather | bytes 1179648 | tf_op jit(solution)/shard_map/all_gather | solution.py:93
  98.4 23.9 %all_gather.30 = bf16[768,384]{1,0:T(8,128)(2,1)S(1)} all-gather(bf16[48,384]{1,0:T(8,128)(2,1)S(1)} %copy-done.38), channel_id=1, replica_groups=mesh['fsdp'=16,'tp'=2] {'fsdp'}, dimensions={0}, use_global_device_ids=true | all-gather | bytes 626688 | tf_op jit(solution)/shard_map/all_gather | solution.py:85
  122.3 2.9 fusion.14
  143.7 12.7 %reduce-scatter.6.cloned.1.call-done = f32[256,768]{1,0:T(8,128)} async-done(((f32[512,768]{1,0:T(8,128)}), f32[256,768]{1,0:T(8,128)}) %reduce-scatter.6.cloned.1.call-update) | async-done | bytes 786448 | tf_op jit(solution)/shard_map/reduce_scatter | solution.py:134
  158.8 12.0 %all_gather.31 = bf16[512,768]{1,0:T(8,128)(2,1)S(1)} all-gather(bf16[256,768]{1,0:T(8,128)(2,1)S(1)} %multiply_convert_fusion.3), channel_id=1, replica_groups=mesh['fsdp'=16,'tp'=2] {'tp'}, dimensions={0}, use_global_device_ids=true | all-gather | bytes 1179648 | tf_op jit(solution)/shard_map/all_gather | solution.py:158
  173.6 67.4 %all-gather.6.cloned.1.call-done = bf16[768,4,1536]{2,0,1:T(8,128)(2,1)} async-done(((bf16[48,4,1536]{2,0,1:T(8,128)(2,1)}), bf16[768,4,1536]{2,0,1:T(8,128)(2,1)}) %all-gather.6.cloned.1.call-update) | async-done | bytes 9437200 | tf_op jit(solution)/shard_map/all_gather | solution.py:86
  241.0 6.1 fusion.26
  249.2 11.4 %multiply_convert_fusion.1 = (bf16[4,192,1536]{2,1,0:T(8,128)(2,1)S(1)}, f32[4,192,1536]{2,1,0:T(8,128)}) fusion(f32[4,192,1536]{2,1,0:T(8,128)S(1)} %get-tuple-element.52, u8[192,1536]{1,0:T(8,128)(4,1)S(1)} %get-tuple-element.23, u8[192,1536]{1,0:T(8,128)(4,1)S(1)} %get-tuple-element.22), kind=kLoop, calls=%fused_computation.24 | loop fusion | flops 82575360 | bytes 12386304 | tf_op jit(solution)/shard_map/convert_element_type | solution.py:171
  260.6 62.4 %all-gather.8.cloned.1.call-done = bf16[768,4,1536]{2,0,1:T(8,128)(2,1)} async-done(((bf16[48,4,1536]{2,0,1:T(8,128)(2,1)}), bf16[768,4,1536]{2,0,1:T(8,128)(2,1)}) %all-gather.8.cloned.1.call-update) | async-done | bytes 9437200 | tf_op jit(solution)/shard_map/all_gather | solution.py:87
  323.0 6.9 fusion.96
  333.0 38.6 %psum.42 = f32[4]{0:T(128)S(1)} all-reduce(f32[4]{0:T(128)S(1)} %select_reduce_fusion), channel_id=1, replica_groups=mesh['fsdp'=16,'tp'=2] {'fsdp','tp'}, use_global_device_ids=true, to_apply=%region_15.16 | all-reduce | flops 4 | bytes 32 | tf_op jit(solution)/shard_map/psum | solution.py:154
  375.8 11.4 %all_gather.34 = bf16[512,768]{1,0:T(8,128)(2,1)S(1)} all-gather(bf16[256,768]{1,0:T(8,128)(2,1)S(1)} %fusion.56), channel_id=1, replica_groups=mesh['fsdp'=16,'tp'=2] {'tp'}, dimensions={0}, use_global_device_ids=true | all-gather | bytes 1179648 | tf_op jit(solution)/shard_map/all_gather | solution.py:190
  387.2 3.4 gather_fusion.2
  390.6 10.2 %add_convert_fusion = bf16[4,192,1536]{2,1,0:T(8,128)(2,1)S(1)} fusion(f32[4,192,1536]{2,1,0:T(8,128)} %get-tuple-element.40, f32[4,192,1536]{2,1,0:T(8,128)} %copy-done.13, bf16[768,4,1536]{2,0,1:T(8,128)(2,1)} %all-gather.8.cloned.1.call-done, bf16[4,192,768]{2,1,0:T(8,128)(2,1)} %bitcast.116, pred[4,192]{1,0:T(4,128)(4,1)S(1)} %gt.19), kind=kOutput, calls=%fused_computation.23 | convolution fusion | flops 1829044224 | bytes 22414080 | tf_op jit(solution)/shard_map/ecd,def->ecf/dot_general | solution.py:192
  400.8 3.2 fusion.97
  407.2 11.2 %fusion.40 = f32[4,1536,768]{2,1,0:T(8,128)} fusion(bf16[4,192,1536]{2,1,0:T(8,128)(2,1)} %copy-done.3, bf16[4,192,768]{2,1,0:T(8,128)(2,1)} %bitcast.115, pred[4,192]{1,0:T(4,128)(4,1)S(1)} %gt.19), kind=kOutput, calls=%fused_computation.81 | convolution fusion | flops 1812529152 | bytes 22414080 | tf_op jit(solution)/shard_map/ecd,ecf->def/dot_general | solution.py:270
  418.3 18.9 %copy.54 = f32[768,6144]{1,0:T(8,128)} copy(f32[768,6144]{0,1:T(8,128)} %bitcast.110) | data formatting | bytes 37748736 | tf_op jit(solution)/shard_map/reshape | solution.py:288
  437.2 9.3 fusion.42
  446.5 18.8 %copy.55 = f32[768,6144]{1,0:T(8,128)} copy(f32[768,6144]{0,1:T(8,128)} %bitcast.109) | data formatting | bytes 37748736 | tf_op jit(solution)/shard_map/reshape | solution.py:289
  469.3 10.6 %all_gather.35 = bf16[512,768]{1,0:T(8,128)(2,1)S(1)} all-gather(bf16[256,768]{1,0:T(8,128)(2,1)S(1)} %get-tuple-element.48), channel_id=1, replica_groups=mesh['fsdp'=16,'tp'=2] {'tp'}, dimensions={0}, use_global_device_ids=true | all-gather | bytes 1179648 | tf_op jit(solution)/shard_map/all_gather | solution.py:219
  482.0 3.9 fusion.17
  498.0 4.5 fusion.59
  504.9 5.2 copy.52
  510.1 28.1 %pad_maximum_fusion = f32[768,13824]{1,0:T(8,128)} fusion(f32[768,6144]{1,0:T(8,128)} %copy.55, f32[768,6144]{1,0:T(8,128)} %copy.54, f32[768,384]{1,0:T(8,128)} %fusion.98, f32[768,1152]{1,0:T(8,128)} %copy.52), kind=kLoop, calls=%fused_computation.6 | loop fusion | flops 31850496 | bytes 84934656 | tf_op jit(solution)/shard_map/concatenate | solution.py:277
  540.8 7.8 fusion.27
  551.0 40.2 %all-reduce.2 = (f32[4]{0:T(128)S(1)}, f32[768]{0:T(1024)}, f32[768]{0:T(1024)}, f32[32,12]{0,1:T(8,128)}, f32[768,4]{0,1:T(4,128)}) all-reduce(f32[4]{0:T(128)} %get-tuple-element.29, f32[768]{0:T(1024)S(1)} %get-tuple-element.26, f32[768]{0:T(1024)} %get-tuple-element.24, ...), channel_id=1, replica_groups=mesh['fsdp'=16,'tp'=2] {'fsdp','tp'}, use_global_device_ids=true, to_apply=%region_18.19 | all-reduce | flops 4996 | bytes 39968 | tf_op jit(solution)/shard_map/psum | solution.py:154
  593.2 2.9 fusion.47
  596.0 346.0 %reduce-scatter.14.cloned.1.call-done = f32[48,13824]{1,0:T(8,128)} async-done(((f32[768,13824]{1,0:T(8,128)}), f32[48,13824]{1,0:T(8,128)}) %reduce-scatter.14.cloned.1.call-update) | async-done | bytes 2654224 | tf_op jit(solution)/shard_map/reduce_scatter | solution.py:276
  (213 shorter events, 73.3 us)
Async XLA Ops:
  7.2 366.2 %copy-start = (bf16[768,4]{0,1:T(4,128)(2,1)S(1)}, bf16[768,4]{0,1:T(4,128)(2,1)}, u32[]{:S(2)}) copy-start(bf16[768,4]{0,1:T(4,128)(2,1)} %param.21) | copy-start | bytes 18436
  7.2 115.1 %all-gather.4.cloned.1.call-start = ((), (), s32[]{:S(2)}) async-start(), calls=%async_computation.5 | async-start | bytes 1880064 | tf_op jit(solution)/shard_map/all_gather | solution.py:84
  7.9 148.4 %reduce-scatter.6.cloned.1.call-start = ((), (), s32[]{:S(2)}) async-start(), calls=%async_computation.6 | async-start | bytes 2359296 | tf_op jit(solution)/shard_map/reduce_scatter | solution.py:134
  9.1 76.0 %copy-start.36 = (f32[768]{0:T(1024)}, f32[768]{0:T(1024)S(1)}, u32[]{:S(2)}) copy-start(f32[768]{0:T(1024)S(1)} %convert_element_type.191) | copy-start | bytes 9220
  17.7 46.2 %copy-start.49 = (bf16[32,12]{0,1:T(8,128)(2,1)S(1)}, bf16[32,12]{0,1:T(8,128)(2,1)}, u32[]{:S(2)}) copy-start(bf16[32,12]{0,1:T(8,128)(2,1)} %param.20) | copy-start | bytes 2308
  74.5 23.9 %copy-start.38 = (bf16[48,384]{1,0:T(8,128)(2,1)S(1)}, bf16[48,384]{1,0:T(8,128)(2,1)}, u32[]{:S(2)}) copy-start(bf16[48,384]{1,0:T(8,128)(2,1)} %param.19) | copy-start | bytes 110596
  98.4 29.2 %copy-start.29 = (bf16[512,768]{1,0:T(8,128)(2,1)}, bf16[512,768]{1,0:T(8,128)(2,1)S(1)}, u32[]{:S(2)}) copy-start(bf16[512,768]{1,0:T(8,128)(2,1)S(1)} %all_gather.28) | copy-start | bytes 2359300
  132.8 108.2 %all-gather.6.cloned.1.call-start = ((), (), s32[]{:S(2)}) async-start(), calls=%async_computation.7 | async-start | bytes 10027008 | tf_op jit(solution)/shard_map/all_gather | solution.py:86
  133.8 189.2 %all-gather.8.cloned.1.call-start = ((), (), s32[]{:S(2)}) async-start(), calls=%async_computation.8 | async-start | bytes 10027008 | tf_op jit(solution)/shard_map/all_gather | solution.py:87
  134.8 238.8 %reduce-scatter.8.cloned.1.call-start = ((), (), s32[]{:S(2)}) async-start(), calls=%async_computation.9 | async-start | bytes 1179648 | tf_op jit(solution)/shard_map/reduce_scatter | solution.py:177
  157.8 310.3 %copy-start.4 = (f32[256,768]{1,0:T(8,128)}, f32[256,768]{1,0:T(8,128)S(1)}, u32[]{:S(2)}) copy-start(f32[256,768]{1,0:T(8,128)S(1)} %get-tuple-element.42) | copy-start | bytes 2359300
  157.8 310.3 %copy-start.39 = (f32[256]{0:T(256)}, f32[256]{0:T(256)S(1)}, u32[]{:S(2)}) copy-start(f32[256]{0:T(256)S(1)} %add_rsqrt_fusion) | copy-start | bytes 3076
  173.6 73.5 %copy-start.9 = (bf16[768,768]{1,0:T(8,128)(2,1)}, bf16[768,768]{1,0:T(8,128)(2,1)S(1)}, u32[]{:S(2)}) copy-start(bf16[768,768]{1,0:T(8,128)(2,1)S(1)} %gather_fusion) | copy-start | bytes 3538948
  260.6 69.3 %copy-start.5 = (bf16[4,192,1536]{2,1,0:T(8,128)(2,1)}, bf16[4,192,1536]{2,1,0:T(8,128)(2,1)S(1)}, u32[]{:S(2)}) copy-start(bf16[4,192,1536]{2,1,0:T(8,128)(2,1)S(1)} %get-tuple-element.39) | copy-start | bytes 7077892
  329.9 43.4 %copy-start.16 = (bf16[256,768]{1,0:T(8,128)(2,1)S(1)}, bf16[256,768]{1,0:T(8,128)(2,1)}, u32[]{:S(2)}) copy-start(bf16[256,768]{1,0:T(8,128)(2,1)} %copy-done.15) | copy-start | bytes 1179652
  330.0 43.6 %copy-start.11 = (bf16[256,768]{1,0:T(8,128)(2,1)S(1)}, bf16[256,768]{1,0:T(8,128)(2,1)}, u32[]{:S(2)}) copy-start(bf16[256,768]{1,0:T(8,128)(2,1)} %param.15) | copy-start | bytes 1179652
  332.8 132.5 %reduce-scatter.10.cloned.1.call-start = ((), (), s32[]{:S(2)}) async-start(), calls=%async_computation.10 | async-start | bytes 2359296 | tf_op jit(solution)/shard_map/reduce_scatter | solution.py:204
  332.8 132.5 %copy-start.43 = (s32[256,1]{0,1:T(1,128)}, s32[256,1]{0,1:T(1,128)S(1)}, u32[]{:S(2)}) copy-start(s32[256,1]{0,1:T(1,128)S(1)} %constant_dynamic-slice_fusion) | copy-start | bytes 3076
  373.3 92.0 %copy-start.46 = (f32[4]{0:T(128)}, f32[4]{0:T(128)S(1)}, u32[]{:S(2)}) copy-start(f32[4]{0:T(128)S(1)} %get-tuple-element.37) | copy-start | bytes 52
  374.9 90.4 %copy-start.44 = (f32[256]{0:T(256)}, f32[256]{0:T(256)S(1)}, u32[]{:S(2)}) copy-start(f32[256]{0:T(256)S(1)} %fusion.58) | copy-start | bytes 3076
  375.6 89.8 %copy-start.42 = (f32[256,4]{0,1:T(4,128)}, f32[256,4]{0,1:T(4,128)S(1)}, u32[]{:S(2)}) copy-start(f32[256,4]{0,1:T(4,128)S(1)} %get-tuple-element.36) | copy-start | bytes 12292
  375.6 89.8 %copy-start.47 = (f32[256]{0:T(256)}, f32[256]{0:T(256)S(1)}, u32[]{:S(2)}) copy-start(f32[256]{0:T(256)S(1)} %get-tuple-element.28) | copy-start | bytes 3076
  406.9 142.6 %reduce-scatter.12.cloned.1.call-start = ((), (), s32[]{:S(2)}) async-start(), calls=%async_computation.11 | async-start | bytes 1179648 | tf_op jit(solution)/shard_map/reduce_scatter | solution.py:262
  407.1 78.8 %copy-start.35 = (f32[6,512]{1,0:T(8,128)}, f32[6,512]{1,0:T(8,128)S(1)}, u32[]{:S(2)}) copy-start(f32[6,512]{1,0:T(8,128)S(1)} %log_add_fusion) | copy-start | bytes 36868
  418.3 18.9 %copy-start.6 = (bf16[4,192,1536]{2,1,0:T(8,128)(2,1)S(1)}, bf16[4,192,1536]{2,1,0:T(8,128)(2,1)}, u32[]{:S(2)}) copy-start(bf16[4,192,1536]{2,1,0:T(8,128)(2,1)} %copy-done.5) | copy-start | bytes 7077892
  446.5 21.5 %copy-start.12 = (bf16[256,768]{1,0:T(8,128)(2,1)S(1)}, bf16[256,768]{1,0:T(8,128)(2,1)}, u32[]{:S(2)}) copy-start(bf16[256,768]{1,0:T(8,128)(2,1)} %param.15) | copy-start | bytes 1179652
  446.5 21.6 %copy-start.28 = (bf16[256,768]{1,0:T(8,128)(2,1)S(1)}, bf16[256,768]{1,0:T(8,128)(2,1)}, u32[]{:S(2)}) copy-start(bf16[256,768]{1,0:T(8,128)(2,1)} %reduce-scatter.8.cloned.1.call-done) | copy-start | bytes 1179652
  465.3 14.5 %copy-start.23 = (bf16[768,384]{1,0:T(8,128)(2,1)S(1)}, bf16[768,384]{1,0:T(8,128)(2,1)}, u32[]{:S(2)}) copy-start(bf16[768,384]{1,0:T(8,128)(2,1)} %copy-done.22) | copy-start | bytes 1769476
  465.3 15.1 %copy-start.27 = (bf16[6,512,64]{1,2,0:T(8,128)(2,1)S(1)}, bf16[6,512,64]{1,2,0:T(8,128)(2,1)}, u32[]{:S(2)}) copy-start(bf16[6,512,64]{1,2,0:T(8,128)(2,1)} %copy-done.26) | copy-start | bytes 1179652
  465.3 20.6 %slice-start = ((s8[6291456]{0:T(1024)(128)(4,1)}), s8[4194304]{0:T(1024)(128)(4,1)S(1)}, s32[]{:S(2)}) async-start(s8[6291456]{0:T(1024)(128)(4,1)} %bitcast.107), calls=%async_computation.13 | async-start | bytes 8388608
  468.0 17.9 %copy-start.45 = (f32[256]{0:T(256)}, f32[256]{0:T(256)S(1)}, u32[]{:S(2)}) copy-start(f32[256]{0:T(256)S(1)} %broadcast_multiply_fusion.1) | copy-start | bytes 3076
  504.6 437.4 %reduce-scatter.14.cloned.1.call-start = ((), (), s32[]{:S(2)}) async-start(), calls=%async_computation.12 | async-start | bytes 45121536 | tf_op jit(solution)/shard_map/reduce_scatter | solution.py:276
  (34 other events, 173.3 us)
Sparse Core Ops, SparseCore 0:
  10.3 43.0 all-gather.3
  132.9 23.3 reduce-scatter.5
  159.5 81.4 all-gather.5
  243.4 79.6 all-gather.7
  332.9 16.1 reduce-scatter.7
  407.0 25.3 reduce-scatter.9
  504.7 16.3 reduce-scatter.11
  538.3 403.6 reduce-scatter.13
where the time goes:
time: 964 us; the launch traced here: 958 us
  waiting for transfers between devices  489 us (51%)
  blocking collectives  149 us (15%)
  local copies, waits for them, and re-layouts  137 us (14%)
  matrix products  94.5 us (10%)
  other arithmetic  68.9 us (7%)
  between operations  17.9 us (2%)
    reduce_scatter x1, waiting for transfers between devices, per_device(): lax.psum_scatter(jnp.concatenate([jnp.concatenate([qkv_term.reshape(shard...  346 us
    psum x2, blocking collectives, per_device(): counts_all, prob_all = lax.psum((counts_local, prob_local), ('fsdp', 'tp'))  78.8 us
    all_gather x1, waiting for transfers between devices, per_device(): lax.all_gather(w_in, 'fsdp', axis=0, tiled=True)  67.4 us
    all_gather x1, waiting for transfers between devices, per_device(): lax.all_gather(w_out, 'fsdp', axis=0, tiled=True)  62.4 us
    eq x1, local copies, waits for them, and re-layouts, bucket_table(): buckets[:, :, None] == bucket_ids[None, None, :]  46.2 us
    concatenate x1, other arithmetic, per_device(): jnp.concatenate([jnp.concatenate([qkv_term.reshape(shard_rows * lax.axis_...  28.1 us
    all_gather x1, blocking collectives, per_device(): lax.all_gather(out_weight, 'fsdp', axis=0, tiled=True)  23.9 us
  transfers between devices with their start and end apart: 8, of which 4 were waited for; matrix products, arithmetic and copies ran while one was open for 23% of the time, Pallas kernels for 0%

commit v1 on v0

v1 whole, which is shorter than its diff:
```python
import math

import jax
import jax.numpy as jnp
from jax import lax
from jax.experimental import pallas as pl
from jax.experimental.pallas import tpu as pltpu
from jax.sharding import PartitionSpec as P

HEADS = 12
HD = 64
BUCKETS = 32
EXP = 4


epsilon = 1e-06
balance_weight = 0.01
far_edges = (12, 16, 23, 32, 46, 64, 91)
highest = lax.Precision.HIGHEST


def bucket_index(query_pos, key_pos):
    offset = key_pos[None, :] - query_pos[:, None]
    spread = jnp.abs(offset)
    far_bucket = 8 + sum(((spread >= edge).astype(jnp.int32) for edge in far_edges))
    near_bucket = jnp.where(spread < 8, spread, far_bucket)
    return near_bucket + jnp.where(offset > 0, 16, 0).astype(jnp.int32)


def norm_rows(values, gain_vec):
    factor = lax.rsqrt(jnp.mean(values * values, axis=-1, keepdims=True) + epsilon)
    hat_rows = values * factor
    return (hat_rows, factor, (hat_rows * gain_vec).astype(jnp.bfloat16))


def norm_back(grad_normed, hat_rows, factor, gain_vec):
    grad_hat = grad_normed * gain_vec
    inner = jnp.mean(grad_hat * hat_rows, axis=-1, keepdims=True)
    return (factor * (grad_hat - hat_rows * inner), jnp.sum(grad_normed * hat_rows, axis=0))


PAIR = 2 * HD
vmem_bytes = 40 * 1024 * 1024


def offset_buckets(seq_len):
    places = jnp.arange(2 * seq_len, dtype=jnp.int32)
    offset = jnp.where(places < seq_len, places, places - 2 * seq_len)
    return bucket_index(jnp.zeros((1,), jnp.int32), offset)[0]


def attn_forward_kernel(len_ref, query_ref, key_ref, value_ref, table_ref, context_ref, probs_ref):
    seq_len = query_ref.shape[0]
    key_pos = lax.broadcasted_iota(jnp.int32, (1, seq_len), 1)
    key_valid = key_pos < len_ref[0]
    parts = []
    for half in range(2):
        cols = slice(half * HD, (half + 1) * HD)
        scores = lax.dot_general(
            query_ref[:, cols],
            key_ref[:, cols],
            (((1,), (1,)), ((), ())),
            preferred_element_type=jnp.float32,
        )
        row = jnp.broadcast_to(table_ref[0, half : half + 1, :], (seq_len, 2 * seq_len))
        bias = pltpu.roll(row, 0, 1, stride=1, stride_axis=0)[:, :seq_len]
        masked = jnp.where(key_valid, scores * (1.0 / math.sqrt(HD)) + bias, -jnp.inf)
        exp_scores = jnp.exp(masked - jnp.max(masked, axis=-1, keepdims=True))
        probs = exp_scores * (1.0 / jnp.sum(exp_scores, axis=-1, keepdims=True))
        probs_ref[half] = probs
        parts.append(
            jnp.dot(
                probs.astype(jnp.bfloat16), value_ref[:, cols], preferred_element_type=jnp.float32
            ).astype(jnp.bfloat16)
        )
    context_ref[...] = jnp.concatenate(parts, axis=1)


def attn_forward(length, qkv, table):
    seq_len = qkv.shape[0]
    head_width = qkv.shape[1] // 3
    pairs = head_width // PAIR

    def column(kind):
        return pl.BlockSpec((seq_len, PAIR), lambda p: (0, kind * pairs + p))

    return pl.pallas_call(
        attn_forward_kernel,
        grid=(pairs,),
        out_shape=(
            jax.ShapeDtypeStruct((seq_len, head_width), jnp.bfloat16),
            jax.ShapeDtypeStruct((2 * pairs, seq_len, seq_len), jnp.float32),
        ),
        in_specs=[
            pl.BlockSpec(memory_space=pltpu.SMEM),
            column(0),
            column(1),
            column(2),
            pl.BlockSpec((1, 2, 2 * seq_len), lambda p: (p, 0, 0)),
        ],
        out_specs=(
            pl.BlockSpec((seq_len, PAIR), lambda p: (0, p)),
            pl.BlockSpec((2, seq_len, seq_len), lambda p: (p, 0, 0)),
        ),
        compiler_params=pltpu.CompilerParams(vmem_limit_bytes=vmem_bytes),
        cost_estimate=pl.CostEstimate(
            flops=8 * pairs * seq_len * seq_len * HD,
            bytes_accessed=8 * pairs * seq_len * seq_len,
            transcendentals=2 * pairs * seq_len * seq_len,
        ),
        name="attn_forward",
    )(length, qkv, qkv, qkv, table.reshape(pairs, 2, 2 * seq_len))


def attn_backward_kernel(
    query_ref, key_ref, value_ref, grad_ref, probs_ref, dq_ref, dk_ref, dv_ref, diag_ref
):
    seq_len = query_ref.shape[0]
    row_id = lax.broadcasted_iota(jnp.int32, (seq_len, seq_len), 0)
    col_id = lax.broadcasted_iota(jnp.int32, (seq_len, seq_len), 1)
    flip = (row_id + col_id == seq_len - 1).astype(jnp.bfloat16)
    scale = 1.0 / math.sqrt(HD)
    query_grads, key_grads, value_grads = [], [], []
    for half in range(2):
        cols = slice(half * HD, (half + 1) * HD)
        grad_context = grad_ref[:, cols]
        probs = probs_ref[half]
        value_grads.append(
            lax.dot_general(
                probs.astype(jnp.bfloat16),
                grad_context,
                (((0,), (0,)), ((), ())),
                preferred_element_type=jnp.float32,
            ).astype(jnp.bfloat16)
        )
        grad_p = lax.dot_general(
            grad_context,
            value_ref[:, cols],
            (((1,), (1,)), ((), ())),
            preferred_element_type=jnp.float32,
        )
        grad_scores = (
            probs * (grad_p - jnp.sum(probs * grad_p, axis=-1, keepdims=True))
        ).astype(jnp.bfloat16)
        query_grads.append(
            (
                jnp.dot(grad_scores, key_ref[:, cols], preferred_element_type=jnp.float32) * scale
            ).astype(jnp.bfloat16)
        )
        key_grads.append(
            (
                lax.dot_general(
                    grad_scores,
                    query_ref[:, cols],
                    (((0,), (0,)), ((), ())),
                    preferred_element_type=jnp.float32,
                )
                * scale
            ).astype(jnp.bfloat16)
        )
        reversed_cols = jnp.dot(grad_scores, flip, preferred_element_type=jnp.float32)
        wide = jnp.concatenate([reversed_cols, jnp.zeros_like(reversed_cols)], axis=1)
        skewed = pltpu.roll(wide, 0, 1, stride=1, stride_axis=0)
        diag_ref[0, half : half + 1, :] = jnp.sum(skewed, axis=0, keepdims=True)
    dq_ref[...] = jnp.concatenate(query_grads, axis=1)
    dk_ref[...] = jnp.concatenate(key_grads, axis=1)
    dv_ref[...] = jnp.concatenate(value_grads, axis=1)


def attn_backward(qkv, grad_context, probs):
    seq_len, head_width = grad_context.shape
    pairs = head_width // PAIR

    def column(kind):
        return pl.BlockSpec((seq_len, PAIR), lambda p: (0, kind * pairs + p))

    rows = jax.ShapeDtypeStruct((seq_len, head_width), jnp.bfloat16)
    dq, dk, dv, diag = pl.pallas_call(
        attn_backward_kernel,
        grid=(pairs,),
        out_shape=(rows, rows, rows, jax.ShapeDtypeStruct((pairs, 2, 2 * seq_len), jnp.float32)),
        in_specs=[
            column(0),
            column(1),
            column(2),
            column(0),
            pl.BlockSpec((2, seq_len, seq_len), lambda p: (p, 0, 0)),
        ],
        out_specs=(
            column(0),
            column(0),
            column(0),
            pl.BlockSpec((1, 2, 2 * seq_len), lambda p: (p, 0, 0)),
        ),
        compiler_params=pltpu.CompilerParams(vmem_limit_bytes=vmem_bytes),
        cost_estimate=pl.CostEstimate(
            flops=24 * pairs * seq_len * seq_len * HD,
            bytes_accessed=8 * pairs * seq_len * seq_len,
            transcendentals=0,
        ),
        name="attn_backward",
    )(qkv, qkv, qkv, grad_context, probs)
    return dq, dk, dv, diag.reshape(2 * pairs, 2 * seq_len)


def outer_kernel(left_ref, right_ref, out_ref):
    out_ref[...] = lax.dot_general(
        left_ref[...],
        right_ref[...],
        (((0,), (0,)), ((), ())),
        preferred_element_type=jnp.float32,
    ).astype(out_ref.dtype)


def expert_outer(left, right):
    rows, width = left.shape
    capacity = rows // EXP
    hidden = right.shape[1]
    tile = math.gcd(hidden, 768)
    tiles = hidden // tile
    return pl.pallas_call(
        outer_kernel,
        grid=(EXP, tiles),
        out_shape=jax.ShapeDtypeStruct((width, EXP * hidden), jnp.bfloat16),
        in_specs=[
            pl.BlockSpec((capacity, width), lambda e, t: (e, 0)),
            pl.BlockSpec((capacity, tile), lambda e, t: (e, t)),
        ],
        out_specs=pl.BlockSpec((width, tile), lambda e, t: (0, e * tiles + t)),
        compiler_params=pltpu.CompilerParams(vmem_limit_bytes=vmem_bytes),
        cost_estimate=pl.CostEstimate(
            flops=2 * rows * width * hidden,
            bytes_accessed=2 * (rows * (width + tiles * hidden) + width * EXP * hidden),
            transcendentals=0,
        ),
        name="expert_outer",
    )(left, right)


def gather_rows(shard):
    return lax.all_gather(shard, "fsdp", axis=0, tiled=True)


def scatter_rows(term):
    return lax.psum_scatter(term, "fsdp", scatter_dimension=0, tiled=True).astype(jnp.float32)


def per_device(
    tokens,
    lengths,
    routes,
    cotangent,
    gain_attn,
    gain_moe,
    qkv_weight,
    out_weight,
    rel_table,
    router_weight,
    w_in,
    w_out,
):
    tok_dev, model_width = tokens.shape
    tp_count = lax.axis_size("tp")
    seq_len = tok_dev * tp_count
    capacity = 3 * seq_len // 8
    slot_count = EXP * capacity
    heads_local = HEADS // tp_count
    hidden_local = w_in.shape[2]
    head_width = qkv_weight.shape[2]
    shard_rows = qkv_weight.shape[0]
    tp_index = lax.axis_index("tp")
    group_id = lax.axis_index("fsdp")
    length = lax.dynamic_index_in_dim(lengths, group_id, 0, keepdims=False)
    all_pos = jnp.arange(seq_len, dtype=jnp.int32)
    key_valid = all_pos < length
    local_pos = tp_index * tok_dev + jnp.arange(tok_dev, dtype=jnp.int32)
    local_valid = (local_pos < length).astype(jnp.float32)[:, None]
    expert_ids = jnp.arange(EXP, dtype=jnp.int32)
    routes_group = routes[:, 0]
    chosen = (routes_group[:, None] == expert_ids[None, :]).astype(jnp.int32) * key_valid.astype(
        jnp.int32
    )[:, None]
    own_counts = jnp.sum(chosen, axis=0).astype(jnp.bfloat16)
    small_shard = jnp.concatenate(
        [
            qkv_weight.reshape(shard_rows, 3 * head_width),
            out_weight,
            jnp.broadcast_to(jnp.pad(own_counts, (0, 128 - EXP))[None, :], (shard_rows, 128)),
        ],
        axis=1,
    )
    small_full = gather_rows(small_shard)
    qkv_full = small_full[:, : 3 * head_width]
    out_full = small_full[:, 3 * head_width : 4 * head_width]
    counts_all = jnp.sum(
        small_full[::shard_rows, 4 * head_width : 4 * head_width + EXP].astype(jnp.float32), axis=0
    )
    in_full = gather_rows(w_in)
    down_full = gather_rows(w_out)
    token_f = tokens.astype(jnp.float32)
    gain_one = gain_attn.astype(jnp.float32)
    gain_two = gain_moe.astype(jnp.float32)
    hat_attn, factor_attn, normed_attn = norm_rows(token_f, gain_one)
    attn_in = lax.all_gather(normed_attn, "tp", axis=0, tiled=True)
    qkv = jnp.dot(attn_in, qkv_full, preferred_element_type=jnp.float32).astype(jnp.bfloat16)
    table_local = lax.dynamic_slice_in_dim(rel_table, tp_index * heads_local, heads_local, 1)
    place_onehot = (
        offset_buckets(seq_len)[:, None] == jnp.arange(BUCKETS, dtype=jnp.int32)[None, :]
    )
    offset_table = jnp.einsum(
        "bh,mb->hm",
        table_local,
        place_onehot.astype(jnp.bfloat16),
        preferred_element_type=jnp.float32,
    )
    context_flat, attn_probs = attn_forward(
        jnp.reshape(length, (1,)).astype(jnp.int32), qkv, offset_table
    )
    attn_sum = lax.psum_scatter(
        lax.dot_general(
            context_flat, out_full, (((1,), (1,)), ((), ())), preferred_element_type=jnp.float32
        ),
        "tp",
        scatter_dimension=0,
        tiled=True,
    )
    mid = token_f + attn_sum * local_valid
    hat_moe, factor_moe, normed_moe = norm_rows(mid, gain_two)
    router_f = router_weight.astype(jnp.float32)
    logits = jnp.dot(normed_moe, router_weight, preferred_element_type=jnp.float32)
    router_probs = jax.nn.softmax(logits, axis=-1)
    route_local = lax.dynamic_slice_in_dim(routes_group, tp_index * tok_dev, tok_dev)
    onehot_local = (route_local[:, None] == expert_ids[None, :]).astype(jnp.float32)
    gate = jnp.sum(router_probs * onehot_local, axis=1, keepdims=True)
    prob_local = jnp.sum(local_valid * router_probs, axis=0)
    total_tokens = jnp.sum(lengths).astype(jnp.float32)
    fraction = counts_all / total_tokens
    grad_out = cotangent.astype(jnp.float32)
    scaled_grad = (grad_out * gate * local_valid).astype(jnp.bfloat16)
    moe_rows = lax.all_gather(
        jnp.concatenate([normed_moe, scaled_grad], axis=1), "tp", axis=0, tiled=True
    )
    slot_ids = jnp.sum(chosen * (jnp.cumsum(chosen, axis=0) - 1), axis=1)
    flat_index = jnp.where(key_valid, routes_group * capacity + slot_ids, slot_count)
    owner = jnp.zeros((slot_count + 1,), jnp.int32).at[flat_index].set(all_pos)[:slot_count]
    filled = (jnp.zeros((slot_count + 1,), jnp.int32).at[flat_index].set(1)[:slot_count] > 0)[
        :, None
    ]
    zero_bf = jnp.zeros((), jnp.bfloat16)
    slot_rows = jnp.where(filled, moe_rows[owner], zero_bf)
    dispatched_flat = slot_rows[:, :model_width]
    grad_expert_flat = slot_rows[:, model_width:]
    dispatched = dispatched_flat.reshape(EXP, capacity, model_width)
    grad_expert = grad_expert_flat.reshape(EXP, capacity, model_width)
    pre_act = jnp.einsum("ecd,def->ecf", dispatched, in_full, preferred_element_type=jnp.float32)
    act = jax.nn.gelu(pre_act, approximate=False).astype(jnp.bfloat16)
    expert_part = jnp.einsum("ecf,def->ecd", act, down_full, preferred_element_type=jnp.float32)
    padded_part = jnp.concatenate(
        [expert_part.reshape(slot_count, model_width), jnp.zeros((1, model_width), jnp.float32)],
        axis=0,
    )
    combined = lax.psum_scatter(
        padded_part[flat_index].astype(jnp.bfloat16), "tp", scatter_dimension=0, tiled=True
    ).astype(jnp.float32)
    mixed = (mid + gate * combined * local_valid).astype(jnp.bfloat16)
    grad_gate = jnp.sum(grad_out * combined * local_valid, axis=1, keepdims=True)
    down_sum = scatter_rows(
        expert_outer(grad_expert_flat, act.reshape(slot_count, hidden_local))
    )
    grad_act = jnp.einsum(
        "ecd,def->ecf", grad_expert, down_full, preferred_element_type=jnp.float32
    )
    _, gelu_pull = jax.vjp(lambda inner_value: jax.nn.gelu(inner_value, approximate=False), pre_act)
    grad_pre = gelu_pull(grad_act)[0].astype(jnp.bfloat16)
    in_sum = scatter_rows(
        expert_outer(dispatched_flat, grad_pre.reshape(slot_count, hidden_local))
    )
    grad_dispatch = jnp.einsum(
        "ecf,def->ecd", grad_pre, in_full, preferred_element_type=jnp.float32
    )
    padded_dispatch = jnp.concatenate(
        [grad_dispatch.reshape(slot_count, model_width), jnp.zeros((1, model_width), jnp.float32)],
        axis=0,
    )
    grad_normed = lax.psum_scatter(
        padded_dispatch[flat_index], "tp", scatter_dimension=0, tiled=True
    )
    aux_grad = balance_weight * EXP * fraction / total_tokens
    grad_probs = onehot_local * grad_gate + local_valid * aux_grad[None, :]
    grad_logits = router_probs * (
        grad_probs - jnp.sum(router_probs * grad_probs, axis=1, keepdims=True)
    )
    grad_router = jnp.einsum(
        "sd,se->de", normed_moe.astype(jnp.float32), grad_logits, precision=highest
    )
    grad_normed = grad_normed + jnp.einsum("se,de->sd", grad_logits, router_f, precision=highest)
    grad_mid_norm, grad_gain_moe = norm_back(grad_normed, hat_moe, factor_moe, gain_two)
    grad_mid = grad_out + grad_mid_norm
    grad_branch = (grad_mid * local_valid).astype(jnp.bfloat16)
    grad_branch_all = lax.all_gather(grad_branch, "tp", axis=0, tiled=True)
    grad_context = jnp.dot(grad_branch_all, out_full, preferred_element_type=jnp.float32).astype(
        jnp.bfloat16
    )
    dq, dk, dv, diag = attn_backward(qkv, grad_context, attn_probs)
    grad_qkv_rows = jnp.concatenate([dq, dk, dv], axis=1)
    grad_attn_part = lax.dot_general(
        grad_qkv_rows, qkv_full, (((1,), (1,)), ((), ())), preferred_element_type=jnp.float32
    )
    back_places = (seq_len - 1 - jnp.arange(2 * seq_len, dtype=jnp.int32)) % (2 * seq_len)
    back_onehot = (
        offset_buckets(seq_len)[back_places][:, None]
        == jnp.arange(BUCKETS, dtype=jnp.int32)[None, :]
    ).astype(jnp.float32)
    grad_table_local = jnp.einsum("hm,mb->hb", diag, back_onehot, precision=highest)
    grad_attn_in = lax.psum_scatter(
        grad_attn_part.astype(jnp.bfloat16), "tp", scatter_dimension=0, tiled=True
    ).astype(jnp.float32)
    grad_token_norm, grad_gain_attn = norm_back(grad_attn_in, hat_attn, factor_attn, gain_one)
    grad_tokens = (grad_mid + grad_token_norm).astype(jnp.bfloat16)
    table_full = lax.dynamic_update_slice(
        jnp.zeros((BUCKETS, HEADS), jnp.float32), grad_table_local.T, (0, tp_index * heads_local)
    )
    qkv_term = jnp.einsum(
        "sd,sc->dc", attn_in, grad_qkv_rows, preferred_element_type=jnp.float32
    ).astype(jnp.bfloat16)
    out_term = jnp.einsum(
        "sj,si->ji", grad_branch_all, context_flat, preferred_element_type=jnp.float32
    ).astype(jnp.bfloat16)
    small_sum = scatter_rows(jnp.concatenate([qkv_term, out_term], axis=1))
    grad_qkv = small_sum[:, : 3 * head_width].reshape(shard_rows, 3, head_width)
    grad_out_shard = small_sum[:, 3 * head_width :]
    grad_in_part = in_sum.reshape(shard_rows, EXP, hidden_local)
    grad_down_part = down_sum.reshape(shard_rows, EXP, hidden_local)
    gain_attn_sum, gain_moe_sum, router_sum, table_sum, prob_all = lax.psum(
        (grad_gain_attn, grad_gain_moe, grad_router, table_full, prob_local), ("fsdp", "tp")
    )
    balance = EXP * jnp.sum(fraction * (prob_all / total_tokens))
    return (
        mixed,
        balance,
        grad_tokens,
        gain_attn_sum,
        gain_moe_sum,
        grad_qkv,
        grad_out_shard,
        table_sum,
        router_sum,
        grad_in_part,
        grad_down_part,
    )


def solution(mesh):
    placed = (
        P(("fsdp", "tp"), None),
        P(),
        P("fsdp", None),
        P(("fsdp", "tp"), None),
        P(),
        P(),
        P("fsdp", None, "tp"),
        P("fsdp", "tp"),
        P(),
        P(),
        P("fsdp", None, "tp"),
        P("fsdp", None, "tp"),
    )
    return jax.shard_map(
        per_device,
        mesh=mesh,
        in_specs=placed,
        out_specs=(
            P(("fsdp", "tp"), None),
            P(),
            P(("fsdp", "tp"), None),
            P(),
            P(),
            P("fsdp", None, "tp"),
            P("fsdp", "tp"),
            P(),
            P(),
            P("fsdp", None, "tp"),
            P("fsdp", None, "tp"),
        ),
        check_vma=False,
    )
```

time: 964 us -> 741 us (0.77)
  blocking collectives: 149 us -> 65.2 us
  local copies, waits for them, and re-layouts: 137 us -> 68.1 us
  matrix products: 94.5 us -> 53.3 us
  other arithmetic: 68.9 us -> 31.4 us
  Pallas kernels: 0 us -> 27 us
  waiting for transfers between devices: 489 us -> 471 us
    reduce_scatter x1 -> x3, waiting for transfers between devices: 346 us -> 230 us  [scatter_rows(): lax.psum_scatter(term, 'fsdp', scatter_dimension=0, tiled=True)]
    all_gather x3 -> x4, waiting for transfers between devices: 130 us -> 194 us  [the longest x3 176 us: gather_rows(): return lax.all_gather(shard, 'fsdp', axis=0, tiled=True)]
    all_gather x3 -> x0, blocking collectives: 47.3 us -> none  [the longest x1 23.9 us: per_device(): lax.all_gather(out_weight, 'fsdp', axis=0, tiled=True)]
    eq x1 -> x0, local copies, waits for them, and re-layouts: 46.2 us -> none  [bucket_table(): buckets[:, :, None] == bucket_ids[None, None, :]]
    dot_general x16 -> x8, matrix products: 73.5 us -> 31.9 us  [the longest x1 15.8 us: per_device(): jnp.einsum('ecd,def->ecf', grad_expert, down_full, preferred_element_type...]
    reshape x6, local copies, waits for them, and re-layouts: 47.1 us -> 7.68 us  [the longest x1 3.01 us: per_device(): grad_down_part = down_sum.reshape(shard_rows, EXP, hidden_local)]
    psum x2 -> x1, blocking collectives: 78.8 us -> 40.9 us  [per_device(): lax.psum((grad_gain_attn, grad_gain_moe, grad_router, table_full, prob_lo...]
    pallas_call x0 -> x4, Pallas kernels: none -> 27 us  [the longest x2 10.3 us: expert_outer(): pl.pallas_call(outer_kernel, grid=(EXP, tiles), out_shape=jax.ShapeDtypeS...]
  transfers between devices with their start and end apart: 8 -> 11, of which waited for: 4 -> 9; matrix products, arithmetic and copies ran while one was open for 23% -> 10% of each run, Pallas kernels for 0% -> 1%
where the time goes in v1:
time: 741 us; the launch traced here: 734 us
  waiting for transfers between devices  471 us (64%)
  local copies, waits for them, and re-layouts  68.1 us (9%)
  blocking collectives  65.2 us (9%)
  matrix products  53.3 us (7%)
  other arithmetic  31.4 us (4%)
  Pallas kernels  27 us (4%)
  between operations  17.7 us (2%)
    reduce_scatter x3, waiting for transfers between devices, scatter_rows(): lax.psum_scatter(term, 'fsdp', scatter_dimension=0, tiled=True)  230 us
    all_gather x3, waiting for transfers between devices, gather_rows(): return lax.all_gather(shard, 'fsdp', axis=0, tiled=True)  176 us
    psum x1, blocking collectives, per_device(): lax.psum((grad_gain_attn, grad_gain_moe, grad_router, table_full, prob_lo...  40.9 us
    unnamed x118, local copies, waits for them, and re-layouts  24.5 us
    reduce_scatter x1, waiting for transfers between devices, per_device(): lax.psum_scatter(lax.dot_general(context_flat, out_full, (((1,), (1,)), (...  24.1 us
    reduce_scatter x1, waiting for transfers between devices, per_device(): lax.psum_scatter(padded_dispatch[flat_index], 'tp', scatter_dimension=0,...  22.2 us
    all_gather x1, waiting for transfers between devices, per_device(): lax.all_gather(jnp.concatenate([normed_moe, scaled_grad], axis=1), 'tp',...  17.7 us
    dot_general x1, matrix products, per_device(): jnp.einsum('ecd,def->ecf', grad_expert, down_full, preferred_element_type...  15.8 us
  transfers between devices with their start and end apart: 11, of which 9 were waited for; matrix products, arithmetic and copies ran while one was open for 10% of the time, Pallas kernels for 1%

profile of v1, /device:TPU:0, one launch (start us, length us, event | category | flops | bytes accessed | tf_op | source)
XLA Modules:
  0.0 733.8 jit_solution(12563426187619158724)
XLA Ops:
  19.5 12.8 %all_gather.18 = bf16[512,768]{1,0:T(8,128)(2,1)S(1)} all-gather(bf16[256,768]{1,0:T(8,128)(2,1)S(1)} %fusion.25), channel_id=1, replica_groups=mesh['fsdp'=16,'tp'=2] {'tp'}, dimensions={0}, use_global_device_ids=true | all-gather | bytes 1179648 | tf_op jit(solution)/shard_map/all_gather | solution.py:304
  32.3 29.0 %all-gather.5.cloned.1.call-done = bf16[768,1664]{1,0:T(8,128)(2,1)} async-done(((bf16[48,1664]{1,0:T(8,128)(2,1)}), bf16[768,1664]{1,0:T(8,128)(2,1)}) %all-gather.5.cloned.1.call-update) | async-done | bytes 2555920 | tf_op jit(solution)/shard_map/all_gather | solution.py:241
  64.0 8.5 %attn_forward.1 = (bf16[512,384]{1,0:T(8,128)(2,1)S(1)}, f32[6,512,512]{2,1,0:T(8,128)S(1)}) custom-call(s32[1]{0:T(128)} %dynamic_slice.10.len_ref, bf16[512,1152]{1,0:T(8,128)(2,1)S(1)} %convolution_convert_fusion.1.query_ref.key_ref.value_ref, bf16[512,1152]{1,0:T(8,128)(2,1)S(1)} %convolution_convert_fusion.1.query_ref.key_ref.value_ref, ...), custom_call_target="tpu_custom_call" | custom-call | flops 402653184 | bytes 6291456 | tf_op jit(solution)/shard_map/attn_forward/pallas_call | solution.py:87
  75.9 2.9 fusion.36
  79.7 24.1 %reduce-scatter.8.cloned.1.call-done = f32[256,768]{1,0:T(8,128)} async-done(((f32[512,768]{1,0:T(8,128)}), f32[256,768]{1,0:T(8,128)}) %reduce-scatter.8.cloned.1.call-update) | async-done | bytes 786448 | tf_op jit(solution)/shard_map/reduce_scatter | solution.py:319
  118.0 17.7 %all-gather.7.cloned.1.call-done = bf16[512,1536]{1,0:T(8,128)(2,1)} async-done(((bf16[256,1536]{1,0:T(8,128)(2,1)}), bf16[512,1536]{1,0:T(8,128)(2,1)}) %all-gather.7.cloned.1.call-update) | async-done | bytes 1572880 | tf_op jit(solution)/shard_map/all_gather | solution.py:340
  135.7 6.9 gather_fusion
  144.7 75.5 %all-gather.9.cloned.1.call-done = bf16[768,4,1536]{2,0,1:T(8,128)(2,1)} async-done(((bf16[48,4,1536]{2,0,1:T(8,128)(2,1)}), bf16[768,4,1536]{2,0,1:T(8,128)(2,1)}) %all-gather.9.cloned.1.call-update) | async-done | bytes 9437200 | tf_op jit(solution)/shard_map/all_gather | solution.py:241
  220.2 10.0 %fusion.17 = (u8[192,1536]{1,0:T(8,128)(4,1)}, u8[192,1536]{1,0:T(8,128)(4,1)}, f32[4,192,1536]{2,1,0:T(8,128)}) fusion(bf16[4,192,768]{2,1,0:T(8,128)(2,1)S(1)} %bitcast.53, bf16[768,4,1536]{2,0,1:T(8,128)(2,1)} %all-gather.9.cloned.1.call-done), kind=kOutput, calls=%fused_computation.49 | convolution fusion | flops 1826684928 | bytes 15925248 | tf_op jit(solution)/shard_map/ecd,def->ecf/dot_general | solution.py:355
  230.2 72.0 %all-gather.11.cloned.1.call-done = bf16[768,4,1536]{2,0,1:T(8,128)(2,1)} async-done(((bf16[48,4,1536]{2,0,1:T(8,128)(2,1)}), bf16[768,4,1536]{2,0,1:T(8,128)(2,1)}) %all-gather.11.cloned.1.call-update) | async-done | bytes 9437200 | tf_op jit(solution)/shard_map/all_gather | solution.py:241
  302.2 15.8 %add_convert_fusion = (bf16[4,192,1536]{2,1,0:T(8,128)(2,1)S(1)}, f32[4,192,1536]{2,1,0:T(8,128)S(1)}) fusion(f32[4,192,1536]{2,1,0:T(8,128)} %get-tuple-element.74, u8[192,1536]{1,0:T(8,128)(4,1)} %get-tuple-element.46, u8[192,1536]{1,0:T(8,128)(4,1)} %get-tuple-element.45, bf16[4,192,768]{2,1,0:T(8,128)(2,1)} %bitcast.54, ...), kind=kOutput, calls=%fused_computation.13 | convolution fusion | flops 1902772224 | bytes 23003136 | tf_op jit(solution)/shard_map/ecd,def->ecf/dot_general | solution.py:370
  321.8 3.2 fusion.70
  326.2 4.9 gather_fusion.1
  331.1 6.9 fusion.71
  339.6 5.0 gather_fusion.2
  352.9 22.2 %reduce-scatter.12.cloned.1.call-done = f32[256,768]{1,0:T(8,128)} async-done(((f32[512,768]{1,0:T(8,128)}), f32[256,768]{1,0:T(8,128)}) %reduce-scatter.12.cloned.1.call-update) | async-done | bytes 786448 | tf_op jit(solution)/shard_map/reduce_scatter | solution.py:385
  375.1 3.0 multiply_reduce_fusion
  378.2 2.8 multiply_convert_fusion.1
  381.0 11.5 %all_gather.23 = bf16[512,768]{1,0:T(8,128)(2,1)S(1)} all-gather(bf16[256,768]{1,0:T(8,128)(2,1)S(1)} %get-tuple-element.70), channel_id=1, replica_groups=mesh['fsdp'=16,'tp'=2] {'tp'}, dimensions={0}, use_global_device_ids=true | all-gather | bytes 1179648 | tf_op jit(solution)/shard_map/all_gather | solution.py:400
  393.4 2.8 copy-done.6
  396.2 8.2 %attn_backward.1 = (bf16[512,384]{1,0:T(8,128)(2,1)S(1)}, bf16[512,384]{1,0:T(8,128)(2,1)S(1)}, bf16[512,384]{1,0:T(8,128)(2,1)S(1)}, f32[3,2,1024]{2,1,0:T(2,128)S(1)}) custom-call(bf16[512,1152]{1,0:T(8,128)(2,1)S(1)} %convolution_convert_fusion.1.query_ref.key_ref.value_ref, bf16[512,1152]{1,0:T(8,128)(2,1)S(1)} %convolution_convert_fusion.1.query_ref.key_ref.value_ref, ...), custom_call_target="tpu_custom_call" | custom-call | flops 1207959552 | bytes 6291456 | tf_op jit(solution)/shard_map/attn_backward/pallas_call | solution.py:178
  415.8 5.0 expert_outer.3
  420.8 3.6 copy-done.1
  425.7 5.3 expert_outer.2
  431.0 3.6 copy-done.2
  435.3 4.5 gather_fusion.3
  442.3 40.9 %all-reduce.3 = (f32[4]{0:T(128)S(1)}, f32[768]{0:T(1024)}, f32[768]{0:T(1024)}, f32[32,12]{0,1:T(8,128)}, f32[768,4]{0,1:T(4,128)}) all-reduce(f32[4]{0:T(128)S(1)} %copy-done.53, f32[768]{0:T(1024)S(1)} %get-tuple-element.49, f32[768]{0:T(1024)S(1)} %copy-done.42, ...), channel_id=1, replica_groups=mesh['fsdp'=16,'tp'=2] {'fsdp','tp'}, use_global_device_ids=true, to_apply=%region_16.17 | all-reduce | flops 4996 | bytes 39968 | tf_op jit(solution)/shard_map/psum | solution.py:434
  486.7 5.8 reduce-scatter.16.cloned.1.call-done
  495.5 111.9 %reduce-scatter.20.cloned.1.call-done = bf16[48,6144]{1,0:T(8,128)(2,1)} async-done(((bf16[768,6144]{1,0:T(8,128)(2,1)}), bf16[48,6144]{1,0:T(8,128)(2,1)}) %reduce-scatter.20.cloned.1.call-update) | async-done | bytes 589840 | tf_op jit(solution)/shard_map/reduce_scatter | solution.py:245
  607.4 3.0 reshape.278
  610.4 112.3 %reduce-scatter.18.cloned.1.call-done = bf16[48,6144]{1,0:T(8,128)(2,1)} async-done(((bf16[768,6144]{1,0:T(8,128)(2,1)}), bf16[48,6144]{1,0:T(8,128)(2,1)}) %reduce-scatter.18.cloned.1.call-update) | async-done | bytes 589840 | tf_op jit(solution)/shard_map/reduce_scatter | solution.py:245
  722.7 3.0 reshape.276
  (211 shorter events, 71.5 us)
Async XLA Ops:
  7.2 99.1 %copy-start = (bf16[768,4]{0,1:T(4,128)(2,1)S(1)}, bf16[768,4]{0,1:T(4,128)(2,1)}, u32[]{:S(2)}) copy-start(bf16[768,4]{0,1:T(4,128)(2,1)} %param.21) | copy-start | bytes 18436
  7.2 54.1 %all-gather.5.cloned.1.call-start = ((), (), s32[]{:S(2)}) async-start(), calls=%async_computation.7 | async-start | bytes 2715648 | tf_op jit(solution)/shard_map/all_gather | solution.py:241
  15.4 88.4 %reduce-scatter.8.cloned.1.call-start = ((), (), s32[]{:S(2)}) async-start(), calls=%async_computation.8 | async-start | bytes 2359296 | tf_op jit(solution)/shard_map/reduce_scatter | solution.py:319
  16.1 16.1 %copy-start.32 = (f32[768]{0:T(1024)}, f32[768]{0:T(1024)S(1)}, u32[]{:S(2)}) copy-start(f32[768]{0:T(1024)S(1)} %convert_element_type.191) | copy-start | bytes 9220
  32.3 29.0 %copy-start.25 = (bf16[512,768]{1,0:T(8,128)(2,1)}, bf16[512,768]{1,0:T(8,128)(2,1)S(1)}, u32[]{:S(2)}) copy-start(bf16[512,768]{1,0:T(8,128)(2,1)S(1)} %all_gather.18) | copy-start | bytes 2359300
  64.0 15.6 %copy-start.39 = (s32[512,1]{0,1:T(1,128)S(1)}, s32[512,1]{0,1:T(1,128)}, u32[]{:S(2)}) copy-start(s32[512,1]{0,1:T(1,128)} %param.14) | copy-start | bytes 6148
  64.0 39.8 %copy-start.16 = (bf16[256,768]{1,0:T(8,128)(2,1)S(1)}, bf16[256,768]{1,0:T(8,128)(2,1)}, u32[]{:S(2)}) copy-start(bf16[256,768]{1,0:T(8,128)(2,1)} %param.12) | copy-start | bytes 1179652
  75.1 32.0 %copy-start.20 = (bf16[256,768]{1,0:T(8,128)(2,1)S(1)}, bf16[256,768]{1,0:T(8,128)(2,1)}, u32[]{:S(2)}) copy-start(bf16[256,768]{1,0:T(8,128)(2,1)} %param.15) | copy-start | bytes 1179652
  78.8 29.6 %copy-start.28 = (bf16[48,4,1536]{2,1,0:T(4,128)(2,1)S(1)}, bf16[48,4,1536]{2,1,0:T(4,128)(2,1)}, u32[]{:S(2)}) copy-start(bf16[48,4,1536]{2,1,0:T(4,128)(2,1)} %param.22) | copy-start | bytes 1769476
  78.8 30.6 %copy-start.29 = (bf16[48,4,1536]{2,1,0:T(4,128)(2,1)S(1)}, bf16[48,4,1536]{2,1,0:T(4,128)(2,1)}, u32[]{:S(2)}) copy-start(bf16[48,4,1536]{2,1,0:T(4,128)(2,1)} %param.23) | copy-start | bytes 1769476
  78.8 56.9 %all-gather.7.cloned.1.call-start = ((), (), s32[]{:S(2)}) async-start(), calls=%async_computation.9 | async-start | bytes 2359296 | tf_op jit(solution)/shard_map/all_gather | solution.py:340
  79.6 30.7 %copy-start.34 = (f32[256]{0:T(256)}, f32[256]{0:T(256)S(1)}, u32[]{:S(2)}) copy-start(f32[256]{0:T(256)S(1)} %compare_convert_fusion) | copy-start | bytes 3076
  79.7 30.7 %copy-start.43 = (s32[256,1]{0,1:T(1,128)}, s32[256,1]{0,1:T(1,128)S(1)}, u32[]{:S(2)}) copy-start(s32[256,1]{0,1:T(1,128)S(1)} %constant_dynamic-slice_fusion) | copy-start | bytes 3076
  108.3 111.9 %all-gather.9.cloned.1.call-start = ((), (), s32[]{:S(2)}) async-start(), calls=%async_computation.10 | async-start | bytes 10027008 | tf_op jit(solution)/shard_map/all_gather | solution.py:241
  109.3 192.9 %all-gather.11.cloned.1.call-start = ((), (), s32[]{:S(2)}) async-start(), calls=%async_computation.11 | async-start | bytes 10027008 | tf_op jit(solution)/shard_map/all_gather | solution.py:241
  110.3 239.2 %reduce-scatter.10.cloned.1.call-start = ((), (), s32[]{:S(2)}) async-start(), calls=%async_computation.12 | async-start | bytes 1179648 | tf_op jit(solution)/shard_map/reduce_scatter | solution.py:362
  144.7 85.5 %copy-start.7 = (bf16[768,768]{1,0:T(8,128)(2,1)}, bf16[768,768]{1,0:T(8,128)(2,1)S(1)}, u32[]{:S(2)}) copy-start(bf16[768,768]{1,0:T(8,128)(2,1)S(1)} %get-tuple-element.68.left_ref) | copy-start | bytes 3538948
  302.2 15.9 %copy-start.22 = (f32[4,192,1536]{2,1,0:T(8,128)S(1)}, f32[4,192,1536]{2,1,0:T(8,128)}, u32[]{:S(2)}) copy-start(f32[4,192,1536]{2,1,0:T(8,128)} %get-tuple-element.74) | copy-start | bytes 14155780
  331.0 44.1 %reduce-scatter.12.cloned.1.call-start = ((), (), s32[]{:S(2)}) async-start(), calls=%async_computation.13 | async-start | bytes 2359296 | tf_op jit(solution)/shard_map/reduce_scatter | solution.py:385
  344.7 96.1 %reduce-scatter.14.cloned.1.call-start = ((), (), s32[]{:S(2)}) async-start(), calls=%async_computation.14 | async-start | bytes 1179648 | tf_op jit(solution)/shard_map/reduce_scatter | solution.py:415
  375.1 17.4 %copy-start.30 = (bf16[768,1664]{1,0:T(8,128)(2,1)S(1)}, bf16[768,1664]{1,0:T(8,128)(2,1)}, u32[]{:S(2)}) copy-start(bf16[768,1664]{1,0:T(8,128)(2,1)} %all-gather.5.cloned.1.call-done) | copy-start | bytes 7667716
  378.2 14.9 %copy-start.18 = (f32[256,768]{1,0:T(8,128)}, f32[256,768]{1,0:T(8,128)S(1)}, u32[]{:S(2)}) copy-start(f32[256,768]{1,0:T(8,128)S(1)} %get-tuple-element.75) | copy-start | bytes 2359300
  378.2 26.2 %copy-start.49 = (f32[256]{0:T(256)}, f32[256]{0:T(256)S(1)}, u32[]{:S(2)}) copy-start(f32[256]{0:T(256)S(1)} %broadcast_multiply_fusion.1) | copy-start | bytes 3076
  408.1 84.4 %reduce-scatter.16.cloned.1.call-start = ((), (), s32[]{:S(2)}) async-start(), calls=%async_computation.15 | async-start | bytes 2506752 | tf_op jit(solution)/shard_map/reduce_scatter | solution.py:245
  414.0 193.4 %reduce-scatter.20.cloned.1.call-start = ((), (), s32[]{:S(2)}) async-start(), calls=%async_computation.17 | async-start | bytes 10027008 | tf_op jit(solution)/shard_map/reduce_scatter | solution.py:245
  424.5 298.2 %reduce-scatter.18.cloned.1.call-start = ((), (), s32[]{:S(2)}) async-start(), calls=%async_computation.16 | async-start | bytes 10027008 | tf_op jit(solution)/shard_map/reduce_scatter | solution.py:245
  434.8 48.4 %copy-start.55 = (f32[4]{0:T(128)S(1)}, f32[4]{0:T(128)}, u32[]{:S(2)}) copy-start(f32[4]{0:T(128)} %get-tuple-element.63) | copy-start | bytes 52
  434.8 49.7 %copy-start.15 = (f32[256,768]{1,0:T(8,128)S(1)}, f32[256,768]{1,0:T(8,128)}, u32[]{:S(2)}) copy-start(f32[256,768]{1,0:T(8,128)} %copy-done.14) | copy-start | bytes 2359300
  434.8 49.7 %copy-start.19 = (f32[256,768]{1,0:T(8,128)S(1)}, f32[256,768]{1,0:T(8,128)}, u32[]{:S(2)}) copy-start(f32[256,768]{1,0:T(8,128)} %copy-done.18) | copy-start | bytes 2359300
  434.8 49.7 %copy-start.21 = (bf16[256,768]{1,0:T(8,128)(2,1)S(1)}, bf16[256,768]{1,0:T(8,128)(2,1)}, u32[]{:S(2)}) copy-start(bf16[256,768]{1,0:T(8,128)(2,1)} %param.15) | copy-start | bytes 1179652
  434.8 49.7 %copy-start.38 = (f32[256]{0:T(256)S(1)}, f32[256]{0:T(256)}, u32[]{:S(2)}) copy-start(f32[256]{0:T(256)} %copy-done.37) | copy-start | bytes 3076
  434.8 49.7 %copy-start.50 = (f32[256]{0:T(256)S(1)}, f32[256]{0:T(256)}, u32[]{:S(2)}) copy-start(f32[256]{0:T(256)} %copy-done.49) | copy-start | bytes 3076
  (36 other events, 162.1 us)
Sparse Core Ops, SparseCore 0:
  15.5 45.6 all-gather.4
  78.9 24.8 reduce-scatter.7
  108.4 27.2 all-gather.6
  138.7 81.4 all-gather.8
  222.6 79.5 all-gather.10
  331.2 15.5 reduce-scatter.9
  349.0 26.0 reduce-scatter.11
  408.2 17.4 reduce-scatter.13
  429.5 62.9 reduce-scatter.15
  497.0 110.3 reduce-scatter.19
  611.5 111.1 reduce-scatter.17

commit v2 on v1

--- a/solution.py
+++ b/solution.py
@@ -212,7 +212,7 @@
     ).astype(out_ref.dtype)
 
 
-def expert_outer(left, right):
+def expert_outer(left, right, first, number):
     rows, width = left.shape
     capacity = rows // EXP
     hidden = right.shape[1]
@@ -220,17 +220,17 @@
     tiles = hidden // tile
     return pl.pallas_call(
         outer_kernel,
-        grid=(EXP, tiles),
-        out_shape=jax.ShapeDtypeStruct((width, EXP * hidden), jnp.bfloat16),
+        grid=(number, tiles),
+        out_shape=jax.ShapeDtypeStruct((width, number * hidden), jnp.bfloat16),
         in_specs=[
-            pl.BlockSpec((capacity, width), lambda e, t: (e, 0)),
-            pl.BlockSpec((capacity, tile), lambda e, t: (e, t)),
+            pl.BlockSpec((capacity, width), lambda e, t: (first + e, 0)),
+            pl.BlockSpec((capacity, tile), lambda e, t: (first + e, t)),
         ],
         out_specs=pl.BlockSpec((width, tile), lambda e, t: (0, e * tiles + t)),
         compiler_params=pltpu.CompilerParams(vmem_limit_bytes=vmem_bytes),
         cost_estimate=pl.CostEstimate(
-            flops=2 * rows * width * hidden,
-            bytes_accessed=2 * (rows * (width + tiles * hidden) + width * EXP * hidden),
+            flops=2 * number * capacity * width * hidden,
+            bytes_accessed=2 * number * (capacity * (width + hidden) + width * hidden),
             transcendentals=0,
         ),
         name="expert_outer",
@@ -241,8 +241,45 @@
     return lax.all_gather(shard, "fsdp", axis=0, tiled=True)
 
 
-def scatter_rows(term):
-    return lax.psum_scatter(term, "fsdp", scatter_dimension=0, tiled=True).astype(jnp.float32)
+def halving_masks():
+    bits = lax.axis_size("fsdp").bit_length() - 1
+    near = [1 << bit for bit in range(min(2, bits))]
+    return near + [1 << bit for bit in range(bits - 1, 1, -1)]
+
+
+def send_order(shard_rows):
+    count = lax.axis_size("fsdp")
+    masks = halving_masks()
+    place = jnp.arange(count, dtype=jnp.int32)
+    mask = jnp.zeros_like(place)
+    for step, step_mask in enumerate(masks):
+        bit = (place >> (len(masks) - 1 - step)) & 1
+        mask = mask + bit * step_mask
+    owner = mask ^ lax.axis_index("fsdp")
+    source = (owner[:, None] * shard_rows + jnp.arange(shard_rows, dtype=jnp.int32)).reshape(-1)
+    return (jnp.arange(count * shard_rows, dtype=jnp.int32)[:, None] == source[None, :]).astype(
+        jnp.bfloat16
+    )
+
+
+def in_order(values, order):
+    return jnp.dot(values, order, preferred_element_type=jnp.float32).astype(jnp.bfloat16)
+
+
+def halve_rows(rows, step):
+    count = lax.axis_size("fsdp")
+    masks = halving_masks()
+    half = rows.shape[0] // 2
+    pairs = [(device, device ^ masks[step]) for device in range(count)]
+    arrived = lax.ppermute(rows[half:], "fsdp", pairs)
+    total = rows[:half].astype(jnp.float32) + arrived.astype(jnp.float32)
+    return total if step == len(masks) - 1 else total.astype(jnp.bfloat16)
+
+
+def finish_rows(rows, step):
+    for later in range(step, len(halving_masks())):
+        rows = halve_rows(rows, later)
+    return rows
 
 
 def per_device(
@@ -364,17 +401,23 @@
     ).astype(jnp.float32)
     mixed = (mid + gate * combined * local_valid).astype(jnp.bfloat16)
     grad_gate = jnp.sum(grad_out * combined * local_valid, axis=1, keepdims=True)
-    down_sum = scatter_rows(
-        expert_outer(grad_expert_flat, act.reshape(slot_count, hidden_local))
-    )
+    order = send_order(shard_rows)
+    grad_sent = in_order(grad_expert_flat, order)
+    act_flat = act.reshape(slot_count, hidden_local)
+    halves = (0, EXP // 2)
+    down_terms = [expert_outer(grad_sent, act_flat, first, EXP // 2) for first in halves]
+    down_rows = [halve_rows(term, 0) for term in down_terms]
     grad_act = jnp.einsum(
         "ecd,def->ecf", grad_expert, down_full, preferred_element_type=jnp.float32
     )
     _, gelu_pull = jax.vjp(lambda inner_value: jax.nn.gelu(inner_value, approximate=False), pre_act)
     grad_pre = gelu_pull(grad_act)[0].astype(jnp.bfloat16)
-    in_sum = scatter_rows(
-        expert_outer(dispatched_flat, grad_pre.reshape(slot_count, hidden_local))
-    )
+    dispatched_sent = in_order(dispatched_flat, order)
+    grad_pre_flat = grad_pre.reshape(slot_count, hidden_local)
+    in_terms = [expert_outer(dispatched_sent, grad_pre_flat, first, EXP // 2) for first in halves]
+    in_terms, down_rows, grad_pre = lax.optimization_barrier((in_terms, down_rows, grad_pre))
+    in_rows = [halve_rows(term, 0) for term in in_terms]
+    down_rows = [halve_rows(rows, 1) for rows in down_rows]
     grad_dispatch = jnp.einsum(
         "ecf,def->ecd", grad_pre, in_full, preferred_element_type=jnp.float32
     )
@@ -398,6 +441,10 @@
     grad_mid = grad_out + grad_mid_norm
     grad_branch = (grad_mid * local_valid).astype(jnp.bfloat16)
     grad_branch_all = lax.all_gather(grad_branch, "tp", axis=0, tiled=True)
+    in_rows, down_rows, grad_branch_all = lax.optimization_barrier(
+        (in_rows, down_rows, grad_branch_all)
+    )
+    in_rows = [halve_rows(rows, 1) for rows in in_rows]
     grad_context = jnp.dot(grad_branch_all, out_full, preferred_element_type=jnp.float32).astype(
         jnp.bfloat16
     )
@@ -421,12 +468,14 @@
         jnp.zeros((BUCKETS, HEADS), jnp.float32), grad_table_local.T, (0, tp_index * heads_local)
     )
     qkv_term = jnp.einsum(
-        "sd,sc->dc", attn_in, grad_qkv_rows, preferred_element_type=jnp.float32
+        "sd,sc->dc", in_order(attn_in, order), grad_qkv_rows, preferred_element_type=jnp.float32
     ).astype(jnp.bfloat16)
     out_term = jnp.einsum(
-        "sj,si->ji", grad_branch_all, context_flat, preferred_element_type=jnp.float32
+        "sj,si->ji", in_order(grad_branch_all, order), context_flat, preferred_element_type=jnp.float32
     ).astype(jnp.bfloat16)
-    small_sum = scatter_rows(jnp.concatenate([qkv_term, out_term], axis=1))
+    small_sum = finish_rows(jnp.concatenate([qkv_term, out_term], axis=1), 0)
+    down_sum = jnp.concatenate([finish_rows(rows, 2) for rows in down_rows], axis=1)
+    in_sum = jnp.concatenate([finish_rows(rows, 2) for rows in in_rows], axis=1)
     grad_qkv = small_sum[:, : 3 * head_width].reshape(shard_rows, 3, head_width)
     grad_out_shard = small_sum[:, 3 * head_width :]
     grad_in_part = in_sum.reshape(shard_rows, EXP, hidden_local)

time: 741 us -> 671 us (0.906)
  waiting for transfers between devices: 471 us -> 297 us
  other arithmetic: 31.4 us -> 62.2 us
  blocking collectives: 65.2 us -> 86.2 us
  local copies, waits for them, and re-layouts: 68.1 us -> 88.7 us
  matrix products: 53.3 us -> 68 us
  starting transfers between devices: 0.46 us -> 14.7 us
    reduce_scatter x3 -> x0, waiting for transfers between devices: 230 us -> none  [scatter_rows(): lax.psum_scatter(term, 'fsdp', scatter_dimension=0, tiled=True)]
    ppermute x0 -> x20, waiting for transfers between devices: none -> 81.9 us  [halve_rows(): arrived = lax.ppermute(rows[half:], 'fsdp', pairs)]
    convert_element_type x0 -> x15, other arithmetic: none -> 32.5 us  [halve_rows(): return total if step == len(masks) - 1 else total.astype(jnp.bfloat16)]
    slice x1 -> x20, local copies, waits for them, and re-layouts: 0.21 us -> 22.8 us  [the longest x19 22.5 us: halve_rows(): arrived = lax.ppermute(rows[half:], 'fsdp', pairs)]
    reduce_scatter x1, waiting for transfers between devices: 22.2 us -> 0.01 us  [per_device(): lax.psum_scatter(padded_dispatch[flat_index], 'tp', scatter_dimension=0,...]
    psum x1, blocking collectives: 40.9 us -> 62 us  [per_device(): lax.psum((grad_gain_attn, grad_gain_moe, grad_router, table_full, prob_lo...]
    ppermute x0 -> x20, starting transfers between devices: none -> 14.4 us  [halve_rows(): arrived = lax.ppermute(rows[half:], 'fsdp', pairs)]
    dot_general x2 -> x4, matrix products: 4.23 us -> 12.5 us  [the longest x1 4.64 us: per_device(): jnp.einsum('sd,sc->dc', in_order(attn_in, order), grad_qkv_rows, preferre...]
  transfers between devices with their start and end apart: 11 -> 28, of which waited for: 9 -> 13; matrix products, arithmetic and copies ran while one was open for 10% -> 23% of each run, Pallas kernels for 1% -> 1%
where the time goes in v2:
time: 671 us; the launch traced here: 663 us
  waiting for transfers between devices  297 us (44%)
  local copies, waits for them, and re-layouts  88.7 us (13%)
  blocking collectives  86.2 us (13%)
  matrix products  68 us (10%)
  other arithmetic  62.2 us (9%)
  Pallas kernels  27.3 us (4%)
  between operations  18.1 us (3%)
  starting transfers between devices  14.7 us (2%)
    all_gather x3, waiting for transfers between devices, gather_rows(): return lax.all_gather(shard, 'fsdp', axis=0, tiled=True)  173 us
    ppermute x20, waiting for transfers between devices, halve_rows(): arrived = lax.ppermute(rows[half:], 'fsdp', pairs)  81.9 us
    psum x1, blocking collectives, per_device(): lax.psum((grad_gain_attn, grad_gain_moe, grad_router, table_full, prob_lo...  62 us
    convert_element_type x15, other arithmetic, halve_rows(): return total if step == len(masks) - 1 else total.astype(jnp.bfloat16)  32.5 us
    reduce_scatter x1, waiting for transfers between devices, per_device(): lax.psum_scatter(lax.dot_general(context_flat, out_full, (((1,), (1,)), (...  24.2 us
    slice x19, local copies, waits for them, and re-layouts, halve_rows(): arrived = lax.ppermute(rows[half:], 'fsdp', pairs)  22.5 us
    unnamed x184, local copies, waits for them, and re-layouts  22.1 us
    all_gather x1, waiting for transfers between devices, per_device(): lax.all_gather(jnp.concatenate([normed_moe, scaled_grad], axis=1), 'tp',...  17.7 us
  transfers between devices with their start and end apart: 28, of which 13 were waited for; matrix products, arithmetic and copies ran while one was open for 23% of the time, Pallas kernels for 1%

profile of v2, /device:TPU:0, one launch (start us, length us, event | category | flops | bytes accessed | tf_op | source)
XLA Modules:
  0.0 662.8 jit_solution(17813820082363260254)
XLA Ops:
  19.5 12.8 %all_gather.18 = bf16[512,768]{1,0:T(8,128)(2,1)S(1)} all-gather(bf16[256,768]{1,0:T(8,128)(2,1)S(1)} %fusion.39), channel_id=1, replica_groups=mesh['fsdp'=16,'tp'=2] {'tp'}, dimensions={0}, use_global_device_ids=true | all-gather | bytes 1179648 | tf_op jit(solution)/shard_map/all_gather | solution.py:341
  32.3 29.0 %all-gather.5.cloned.1.call-done = bf16[768,1664]{1,0:T(8,128)(2,1)} async-done(((bf16[48,1664]{1,0:T(8,128)(2,1)}), bf16[768,1664]{1,0:T(8,128)(2,1)}) %all-gather.5.cloned.1.call-update) | async-done | bytes 2555920 | tf_op jit(solution)/shard_map/all_gather | solution.py:241
  64.0 8.5 %attn_forward.1 = (bf16[512,384]{1,0:T(8,128)(2,1)S(1)}, f32[6,512,512]{2,1,0:T(8,128)S(1)}) custom-call(s32[1]{0:T(128)} %dynamic_slice.10.len_ref, bf16[512,1152]{1,0:T(8,128)(2,1)S(1)} %convolution_convert_fusion.1.query_ref.key_ref.value_ref, bf16[512,1152]{1,0:T(8,128)(2,1)S(1)} %convolution_convert_fusion.1.query_ref.key_ref.value_ref, ...), custom_call_target="tpu_custom_call" | custom-call | flops 402653184 | bytes 6291456 | tf_op jit(solution)/shard_map/attn_forward/pallas_call | solution.py:87
  79.6 24.2 %reduce-scatter.5.cloned.1.call-done = f32[256,768]{1,0:T(8,128)} async-done(((f32[512,768]{1,0:T(8,128)}), f32[256,768]{1,0:T(8,128)}) %reduce-scatter.5.cloned.1.call-update) | async-done | bytes 786448 | tf_op jit(solution)/shard_map/reduce_scatter | solution.py:356
  117.9 17.7 %all-gather.7.cloned.1.call-done = bf16[512,1536]{1,0:T(8,128)(2,1)} async-done(((bf16[256,1536]{1,0:T(8,128)(2,1)}), bf16[512,1536]{1,0:T(8,128)(2,1)}) %all-gather.7.cloned.1.call-update) | async-done | bytes 1572880 | tf_op jit(solution)/shard_map/all_gather | solution.py:377
  135.7 7.1 %gather_fusion = bf16[768,1536]{1,0:T(8,128)(2,1)S(1)} fusion(bf16[512,1536]{1,0:T(8,128)(2,1)} %all-gather.7.cloned.1.call-done, s32[1024]{0:T(1024)} %pad_clamp_fusion.1), kind=kCustom, calls=%fused_computation | custom fusion | bytes 4721664 | tf_op jit(solution)/shard_map/gather | solution.py:387
  147.0 72.5 %all-gather.9.cloned.1.call-done = bf16[768,4,1536]{2,0,1:T(8,128)(2,1)} async-done(((bf16[48,4,1536]{2,0,1:T(8,128)(2,1)}), bf16[768,4,1536]{2,0,1:T(8,128)(2,1)}) %all-gather.9.cloned.1.call-update) | async-done | bytes 9437200 | tf_op jit(solution)/shard_map/all_gather | solution.py:241
  219.5 10.1 %fusion.31 = (u8[192,1536]{1,0:T(8,128)(4,1)}, u8[192,1536]{1,0:T(8,128)(4,1)}, f32[4,192,1536]{2,1,0:T(8,128)}) fusion(bf16[4,192,768]{2,1,0:T(8,128)(2,1)S(1)} %bitcast.66, bf16[768,4,1536]{2,0,1:T(8,128)(2,1)} %all-gather.9.cloned.1.call-done), kind=kOutput, calls=%fused_computation.81 | convolution fusion | flops 1826684928 | bytes 15925248 | tf_op jit(solution)/shard_map/ecd,def->ecf/dot_general | solution.py:392
  229.6 72.0 %all-gather.11.cloned.1.call-done = bf16[768,4,1536]{2,0,1:T(8,128)(2,1)} async-done(((bf16[48,4,1536]{2,0,1:T(8,128)(2,1)}), bf16[768,4,1536]{2,0,1:T(8,128)(2,1)}) %all-gather.11.cloned.1.call-update) | async-done | bytes 9437200 | tf_op jit(solution)/shard_map/all_gather | solution.py:241
  301.6 15.8 %add_convert_fusion.4 = (bf16[4,192,1536]{2,1,0:T(8,128)(2,1)S(1)}, f32[4,192,1536]{2,1,0:T(8,128)S(1)}) fusion(f32[4,192,1536]{2,1,0:T(8,128)} %get-tuple-element.94, u8[192,1536]{1,0:T(8,128)(4,1)} %get-tuple-element.66, u8[192,1536]{1,0:T(8,128)(4,1)} %get-tuple-element.65, bf16[4,192,768]{2,1,0:T(8,128)(2,1)} %bitcast.65, ...), kind=kOutput, calls=%fused_computation.17 | convolution fusion | flops 1902772224 | bytes 23003136 | tf_op jit(solution)/shard_map/ecd,def->ecf/dot_general | solution.py:410
  327.6 9.0 %gather_fusion.3 = s32[1024]{0:T(1024)} fusion(s32[1024]{0:T(1024)S(1)} %fusion.57, s32[1024]{0:T(1024)} %get-tuple-element.97), kind=kCustom, calls=%fused_computation.3 | custom fusion | bytes 12288 | tf_op jit(solution)/shard_map/gather | solution.py:458
  349.6 6.9 %fusion.98 = bf16[4,192,768]{2,1,0:T(8,128)(2,1)S(1)} fusion(bf16[4,192,1536]{2,1,0:T(8,128)(2,1)S(1)} %copy-done.3, bf16[768,4,1536]{2,0,1:T(8,128)(2,1)} %all-gather.11.cloned.1.call-done), kind=kOutput, calls=%fused_computation.212 | convolution fusion | flops 1811939328 | bytes 12976128 | tf_op jit(solution)/shard_map/ecf,def->ecd/dot_general | solution.py:394
  357.6 4.5 gather_fusion.1
  370.7 4.2 add_convert_fusion.2
  375.0 4.9 add_convert_fusion.3
  384.3 3.4 slice.169
  391.3 6.9 %fusion.99 = f32[4,192,768]{2,1,0:T(8,128)S(1)} fusion(bf16[4,192,1536]{2,1,0:T(8,128)(2,1)S(1)} %get-tuple-element.28, bf16[768,4,1536]{2,0,1:T(8,128)(2,1)} %all-gather.9.cloned.1.call-done), kind=kOutput, calls=%fused_computation.213 | convolution fusion | flops 1811939328 | bytes 14155776 | tf_op jit(solution)/shard_map/ecf,def->ecd/dot_general | solution.py:421
  399.7 4.9 gather_fusion.2
  412.9 21.7 %collective-permute-done.4 = bf16[192,3072]{1,0:T(8,128)(2,1)} collective-permute-done((bf16[192,3072]{1,0:T(8,128)(2,1)}, bf16[192,3072]{1,0:T(8,128)(2,1)}, u32[]{:S(2)}, u32[]{:S(2)}) %collective-permute-start.4) | collective-permute-done | bytes 1179680 | tf_op jit(solution)/shard_map/ppermute | solution.py:274
  437.2 4.8 add_convert_fusion
  447.7 11.4 %all_gather.23 = bf16[512,768]{1,0:T(8,128)(2,1)} all-gather(bf16[256,768]{1,0:T(8,128)(2,1)S(1)} %get-tuple-element.90), channel_id=1, replica_groups=mesh['fsdp'=16,'tp'=2] {'tp'}, dimensions={0}, use_global_device_ids=true | all-gather | bytes 1179648 | tf_op jit(solution)/shard_map/all_gather | solution.py:443
  459.1 3.5 convolution_convert_fusion.2
  467.3 8.2 %attn_backward.1 = (bf16[512,384]{1,0:T(8,128)(2,1)S(1)}, bf16[512,384]{1,0:T(8,128)(2,1)S(1)}, bf16[512,384]{1,0:T(8,128)(2,1)S(1)}, f32[3,2,1024]{2,1,0:T(2,128)S(1)}) custom-call(bf16[512,1152]{1,0:T(8,128)(2,1)S(1)} %convolution_convert_fusion.1.query_ref.key_ref.value_ref, bf16[512,1152]{1,0:T(8,128)(2,1)S(1)} %convolution_convert_fusion.1.query_ref.key_ref.value_ref, ...), custom_call_target="tpu_custom_call" | custom-call | flops 1207959552 | bytes 6291456 | tf_op jit(solution)/shard_map/attn_backward/pallas_call | solution.py:178
  484.8 4.6 convolution_convert_fusion
  489.5 3.9 fusion.15
  502.1 17.7 %collective-permute-done.18 = bf16[96,3072]{1,0:T(8,128)(2,1)} collective-permute-done((bf16[96,3072]{1,0:T(8,128)(2,1)}, bf16[96,3072]{1,0:T(8,128)(2,1)}, u32[]{:S(2)}, u32[]{:S(2)}) %collective-permute-start.18) | collective-permute-done | bytes 589856 | tf_op jit(solution)/shard_map/ppermute | solution.py:274
  521.3 11.3 %collective-permute-done.16 = bf16[96,3072]{1,0:T(8,128)(2,1)} collective-permute-done((bf16[96,3072]{1,0:T(8,128)(2,1)}, bf16[96,3072]{1,0:T(8,128)(2,1)}, u32[]{:S(2)}, u32[]{:S(2)}) %collective-permute-start.16) | collective-permute-done | bytes 589856 | tf_op jit(solution)/shard_map/ppermute | solution.py:274
  533.9 4.8 collective-permute-done.19
  538.8 6.2 collective-permute-done.17
  562.0 62.0 %all-reduce.3 = (f32[4]{0:T(128)S(1)}, f32[768]{0:T(1024)}, f32[768]{0:T(1024)}, f32[32,12]{0,1:T(8,128)}, f32[768,4]{0,1:T(4,128)}) all-reduce(f32[4]{0:T(128)S(1)} %copy-done.81, f32[768]{0:T(1024)S(1)} %get-tuple-element.69, f32[768]{0:T(1024)S(1)} %get-tuple-element.67, ...), channel_id=1, replica_groups=mesh['fsdp'=16,'tp'=2] {'fsdp','tp'}, use_global_device_ids=true, to_apply=%region_16.17 | all-reduce | flops 4996 | bytes 39968 | tf_op jit(solution)/shard_map/psum | solution.py:483
  632.9 11.6 %collective-permute-done.8 = bf16[96,1536]{1,0:T(8,128)(2,1)S(1)} collective-permute-done((bf16[96,1536]{1,0:T(8,128)(2,1)S(1)}, bf16[96,1536]{1,0:T(8,128)(2,1)S(1)}, u32[]{:S(2)}, u32[]{:S(2)}) %collective-permute-start.8) | collective-permute-done | bytes 294944 | tf_op jit(solution)/shard_map/ppermute | solution.py:274
  645.8 5.4 collective-permute-done.12
  (359 shorter events, 153.2 us)
Async XLA Ops:
  7.2 99.0 %copy-start = (bf16[768,4]{0,1:T(4,128)(2,1)S(1)}, bf16[768,4]{0,1:T(4,128)(2,1)}, u32[]{:S(2)}) copy-start(bf16[768,4]{0,1:T(4,128)(2,1)} %param.21) | copy-start | bytes 18436
  7.2 54.1 %all-gather.5.cloned.1.call-start = ((), (), s32[]{:S(2)}) async-start(), calls=%async_computation.4 | async-start | bytes 2715648 | tf_op jit(solution)/shard_map/all_gather | solution.py:241
  15.4 88.3 %reduce-scatter.5.cloned.1.call-start = ((), (), s32[]{:S(2)}) async-start(), calls=%async_computation.5 | async-start | bytes 2359296 | tf_op jit(solution)/shard_map/reduce_scatter | solution.py:356
  78.8 56.9 %all-gather.7.cloned.1.call-start = ((), (), s32[]{:S(2)}) async-start(), calls=%async_computation.6 | async-start | bytes 2359296 | tf_op jit(solution)/shard_map/all_gather | solution.py:377
  108.3 111.3 %all-gather.9.cloned.1.call-start = ((), (), s32[]{:S(2)}) async-start(), calls=%async_computation.7 | async-start | bytes 10027008 | tf_op jit(solution)/shard_map/all_gather | solution.py:241
  109.3 192.3 %all-gather.11.cloned.1.call-start = ((), (), s32[]{:S(2)}) async-start(), calls=%async_computation.8 | async-start | bytes 10027008 | tf_op jit(solution)/shard_map/all_gather | solution.py:241
  110.3 271.2 %reduce-scatter.7.cloned.1.call-start = ((), (), s32[]{:S(2)}) async-start(), calls=%async_computation.9 | async-start | bytes 1179648 | tf_op jit(solution)/shard_map/reduce_scatter | solution.py:399
  324.1 46.5 %collective-permute-start.1 = (bf16[384,3072]{1,0:T(8,128)(2,1)}, bf16[384,3072]{1,0:T(8,128)(2,1)}, u32[]{:S(2)}, u32[]{:S(2)}) collective-permute-start(bf16[384,3072]{1,0:T(8,128)(2,1)} %slice.220), channel_id=1, source_target_pairs={{0,2},{2,0},{4,6},{6,4},{8,10},{10,8},{12,14},{14,12},{16,18},{18,... | collective-permute-start | bytes 7077896 | tf_op jit(solution)/shard_map/ppermute | solution.py:274
  346.6 28.3 %collective-permute-start = (bf16[384,3072]{1,0:T(8,128)(2,1)}, bf16[384,3072]{1,0:T(8,128)(2,1)}, u32[]{:S(2)}, u32[]{:S(2)}) collective-permute-start(bf16[384,3072]{1,0:T(8,128)(2,1)} %slice.218), channel_id=1, source_target_pairs={{0,2},{2,0},{4,6},{6,4},{8,10},{10,8},{12,14},{14,12},{16,18},{18,... | collective-permute-start | bytes 7077896 | tf_op jit(solution)/shard_map/ppermute | solution.py:274
  362.1 82.3 %reduce-scatter.9.cloned.1.call-start = ((), (), s32[]{:S(2)}) async-start(), calls=%async_computation.10 | async-start | bytes 2359296 | tf_op jit(solution)/shard_map/reduce_scatter | solution.py:428
  380.9 29.1 %collective-permute-start.5 = (bf16[192,3072]{1,0:T(8,128)(2,1)}, bf16[192,3072]{1,0:T(8,128)(2,1)}, u32[]{:S(2)}, u32[]{:S(2)}) collective-permute-start(bf16[192,3072]{1,0:T(8,128)(2,1)} %slice.173), channel_id=1, source_target_pairs={{0,4},{2,6},{4,0},{6,2},{8,12},{10,14},{12,8},{14,10},{16,20},{18,... | collective-permute-start | bytes 3538952 | tf_op jit(solution)/shard_map/ppermute | solution.py:274
  387.7 49.5 %collective-permute-start.3 = (bf16[384,3072]{1,0:T(8,128)(2,1)}, bf16[384,3072]{1,0:T(8,128)(2,1)}, u32[]{:S(2)}, u32[]{:S(2)}) collective-permute-start(bf16[384,3072]{1,0:T(8,128)(2,1)} %slice.169), channel_id=1, source_target_pairs={{0,2},{2,0},{4,6},{6,4},{8,10},{10,8},{12,14},{14,12},{16,18},{18,... | collective-permute-start | bytes 7077896 | tf_op jit(solution)/shard_map/ppermute | solution.py:274
  389.8 44.8 %collective-permute-start.4 = (bf16[192,3072]{1,0:T(8,128)(2,1)}, bf16[192,3072]{1,0:T(8,128)(2,1)}, u32[]{:S(2)}, u32[]{:S(2)}) collective-permute-start(bf16[192,3072]{1,0:T(8,128)(2,1)} %slice.171), channel_id=1, source_target_pairs={{0,4},{2,6},{4,0},{6,2},{8,12},{10,14},{12,8},{14,10},{16,20},{18,... | collective-permute-start | bytes 3538952 | tf_op jit(solution)/shard_map/ppermute | solution.py:274
  404.6 155.9 %reduce-scatter.11.cloned.1.call-start = ((), (), s32[]{:S(2)}) async-start(), calls=%async_computation.11 | async-start | bytes 1179648 | tf_op jit(solution)/shard_map/reduce_scatter | solution.py:462
  406.7 35.4 %collective-permute-start.2 = (bf16[384,3072]{1,0:T(8,128)(2,1)S(1)}, bf16[384,3072]{1,0:T(8,128)(2,1)S(1)}, u32[]{:S(2)}, u32[]{:S(2)}) collective-permute-start(bf16[384,3072]{1,0:T(8,128)(2,1)S(1)} %slice.167), channel_id=1, source_target_pairs={{0,2},{2,0},{4,6},{6,4},{8,10},{10,8},{12,14},{14,12},{16,18},{18,... | collective-permute-start | bytes 7077896 | tf_op jit(solution)/shard_map/ppermute | solution.py:274
  479.6 40.3 %collective-permute-start.18 = (bf16[96,3072]{1,0:T(8,128)(2,1)}, bf16[96,3072]{1,0:T(8,128)(2,1)}, u32[]{:S(2)}, u32[]{:S(2)}) collective-permute-start(bf16[96,3072]{1,0:T(8,128)(2,1)} %slice.201), channel_id=1, source_target_pairs={{0,16},{2,18},{4,20},{6,22},{8,24},{10,26},{12,28},{14,30},{16,0},... | collective-permute-start | bytes 1769480 | tf_op jit(solution)/shard_map/ppermute | solution.py:274
  481.0 51.6 %collective-permute-start.16 = (bf16[96,3072]{1,0:T(8,128)(2,1)}, bf16[96,3072]{1,0:T(8,128)(2,1)}, u32[]{:S(2)}, u32[]{:S(2)}) collective-permute-start(bf16[96,3072]{1,0:T(8,128)(2,1)} %slice.197), channel_id=1, source_target_pairs={{0,16},{2,18},{4,20},{6,22},{8,24},{10,26},{12,28},{14,30},{16,0},... | collective-permute-start | bytes 1769480 | tf_op jit(solution)/shard_map/ppermute | solution.py:274
  498.5 48.4 %collective-permute-start.13 = (bf16[192,3072]{1,0:T(8,128)(2,1)}, bf16[192,3072]{1,0:T(8,128)(2,1)}, u32[]{:S(2)}, u32[]{:S(2)}) collective-permute-start(bf16[192,3072]{1,0:T(8,128)(2,1)} %slice.191), channel_id=1, source_target_pairs={{0,4},{2,6},{4,0},{6,2},{8,12},{10,14},{12,8},{14,10},{16,20},{18,... | collective-permute-start | bytes 3538952 | tf_op jit(solution)/shard_map/ppermute | solution.py:274
  499.0 51.4 %collective-permute-start.10 = (bf16[192,3072]{1,0:T(8,128)(2,1)}, bf16[192,3072]{1,0:T(8,128)(2,1)}, u32[]{:S(2)}, u32[]{:S(2)}) collective-permute-start(bf16[192,3072]{1,0:T(8,128)(2,1)} %slice.185), channel_id=1, source_target_pairs={{0,4},{2,6},{4,0},{6,2},{8,12},{10,14},{12,8},{14,10},{16,20},{18,... | collective-permute-start | bytes 3538952 | tf_op jit(solution)/shard_map/ppermute | solution.py:274
  501.6 55.0 %collective-permute-start.6 = (bf16[384,1536]{1,0:T(8,128)(2,1)}, bf16[384,1536]{1,0:T(8,128)(2,1)}, u32[]{:S(2)}, u32[]{:S(2)}) collective-permute-start(bf16[384,1536]{1,0:T(8,128)(2,1)} %pad_maximum_fusion), channel_id=1, source_target_pairs={{0,2},{2,0},{4,6},{6,4},{8,10},{10,8},{12,14},{14,12},{16,18},{18,... | collective-permute-start | bytes 3538952 | tf_op jit(solution)/shard_map/ppermute | solution.py:274
  521.2 17.6 %collective-permute-start.19 = (bf16[48,3072]{1,0:T(8,128)(2,1)S(1)}, bf16[48,3072]{1,0:T(8,128)(2,1)S(1)}, u32[]{:S(2)}, u32[]{:S(2)}) collective-permute-start(bf16[48,3072]{1,0:T(8,128)(2,1)S(1)} %slice.242), channel_id=1, source_target_pairs={{0,8},{2,10},{4,12},{6,14},{8,0},{10,2},{12,4},{14,6},{16,24},{18,... | collective-permute-start | bytes 884744 | tf_op jit(solution)/shard_map/ppermute | solution.py:274
  533.8 11.1 %collective-permute-start.17 = (bf16[48,3072]{1,0:T(8,128)(2,1)S(1)}, bf16[48,3072]{1,0:T(8,128)(2,1)S(1)}, u32[]{:S(2)}, u32[]{:S(2)}) collective-permute-start(bf16[48,3072]{1,0:T(8,128)(2,1)S(1)} %slice.240), channel_id=1, source_target_pairs={{0,8},{2,10},{4,12},{6,14},{8,0},{10,2},{12,4},{14,6},{16,24},{18,... | collective-permute-start | bytes 884744 | tf_op jit(solution)/shard_map/ppermute | solution.py:274
  550.1 77.5 %collective-permute-start.14 = (bf16[96,3072]{1,0:T(8,128)(2,1)}, bf16[96,3072]{1,0:T(8,128)(2,1)}, u32[]{:S(2)}, u32[]{:S(2)}) collective-permute-start(bf16[96,3072]{1,0:T(8,128)(2,1)} %slice.236), channel_id=1, source_target_pairs={{0,16},{2,18},{4,20},{6,22},{8,24},{10,26},{12,28},{14,30},{16,0},... | collective-permute-start | bytes 1769480 | tf_op jit(solution)/shard_map/ppermute | solution.py:274
  554.0 70.0 %copy-start.83 = (f32[4]{0:T(128)S(1)}, f32[4]{0:T(128)}, u32[]{:S(2)}) copy-start(f32[4]{0:T(128)} %get-tuple-element.83) | copy-start | bytes 52
  554.0 71.3 %copy-start.29 = (f32[256,768]{1,0:T(8,128)S(1)}, f32[256,768]{1,0:T(8,128)}, u32[]{:S(2)}) copy-start(f32[256,768]{1,0:T(8,128)} %copy-done.28) | copy-start | bytes 2359300
  554.0 71.3 %copy-start.32 = (bf16[256,768]{1,0:T(8,128)(2,1)S(1)}, bf16[256,768]{1,0:T(8,128)(2,1)}, u32[]{:S(2)}) copy-start(bf16[256,768]{1,0:T(8,128)(2,1)} %param.15) | copy-start | bytes 1179652
  554.0 77.5 %collective-permute-start.11 = (bf16[96,3072]{1,0:T(8,128)(2,1)}, bf16[96,3072]{1,0:T(8,128)(2,1)}, u32[]{:S(2)}, u32[]{:S(2)}) collective-permute-start(bf16[96,3072]{1,0:T(8,128)(2,1)} %slice.232), channel_id=1, source_target_pairs={{0,16},{2,18},{4,20},{6,22},{8,24},{10,26},{12,28},{14,30},{16,0},... | collective-permute-start | bytes 1769480 | tf_op jit(solution)/shard_map/ppermute | solution.py:274
  560.0 69.2 %collective-permute-start.7 = (bf16[192,1536]{1,0:T(8,128)(2,1)}, bf16[192,1536]{1,0:T(8,128)(2,1)S(1)}, u32[]{:S(2)}, u32[]{:S(2)}) collective-permute-start(bf16[192,1536]{1,0:T(8,128)(2,1)} %slice.224), channel_id=1, source_target_pairs={{0,4},{2,6},{4,0},{6,2},{8,12},{10,14},{12,8},{14,10},{16,20},{18,... | collective-permute-start | bytes 1769480 | tf_op jit(solution)/shard_map/ppermute | solution.py:274
  629.1 16.6 %collective-permute-start.15 = (bf16[48,3072]{1,0:T(8,128)(2,1)S(1)}, bf16[48,3072]{1,0:T(8,128)(2,1)S(1)}, u32[]{:S(2)}, u32[]{:S(2)}) collective-permute-start(bf16[48,3072]{1,0:T(8,128)(2,1)S(1)} %slice.238), channel_id=1, source_target_pairs={{0,8},{2,10},{4,12},{6,14},{8,0},{10,2},{12,4},{14,6},{16,24},{18,... | collective-permute-start | bytes 884744 | tf_op jit(solution)/shard_map/ppermute | solution.py:274
  629.4 15.1 %collective-permute-start.8 = (bf16[96,1536]{1,0:T(8,128)(2,1)S(1)}, bf16[96,1536]{1,0:T(8,128)(2,1)S(1)}, u32[]{:S(2)}, u32[]{:S(2)}) collective-permute-start(bf16[96,1536]{1,0:T(8,128)(2,1)S(1)} %slice.226), channel_id=1, source_target_pairs={{0,16},{2,18},{4,20},{6,22},{8,24},{10,26},{12,28},{14,30},{16,0},... | collective-permute-start | bytes 884744 | tf_op jit(solution)/shard_map/ppermute | solution.py:274
  632.8 18.4 %collective-permute-start.12 = (bf16[48,3072]{1,0:T(8,128)(2,1)S(1)}, bf16[48,3072]{1,0:T(8,128)(2,1)S(1)}, u32[]{:S(2)}, u32[]{:S(2)}) collective-permute-start(bf16[48,3072]{1,0:T(8,128)(2,1)S(1)} %slice.234), channel_id=1, source_target_pairs={{0,8},{2,10},{4,12},{6,14},{8,0},{10,2},{12,4},{14,6},{16,24},{18,... | collective-permute-start | bytes 884744 | tf_op jit(solution)/shard_map/ppermute | solution.py:274
  644.6 8.6 %collective-permute-start.9 = (bf16[48,1536]{1,0:T(8,128)(2,1)S(1)}, bf16[48,1536]{1,0:T(8,128)(2,1)S(1)}, u32[]{:S(2)}, u32[]{:S(2)}) collective-permute-start(bf16[48,1536]{1,0:T(8,128)(2,1)S(1)} %slice.228), channel_id=1, source_target_pairs={{0,8},{2,10},{4,12},{6,14},{8,0},{10,2},{12,4},{14,6},{16,24},{18,... | collective-permute-start | bytes 442376 | tf_op jit(solution)/shard_map/ppermute | solution.py:274
  (86 other events, 626.9 us)
Sparse Core Ops, SparseCore 0:
  15.5 45.6 all-gather.4
  78.9 24.8 reduce-scatter.4
  108.4 27.2 all-gather.6
  138.0 81.4 all-gather.8
  221.9 79.5 all-gather.10
  362.2 15.5 reduce-scatter.6
  404.7 24.1 reduce-scatter.8
  493.6 15.5 reduce-scatter.10

commit v3 on v2

--- a/solution.py
+++ b/solution.py
@@ -280,6 +280,46 @@
     for later in range(step, len(halving_masks())):
         rows = halve_rows(rows, later)
     return rows
+
+
+swap = [(0, 1), (1, 0)]
+
+
+def tp_gather(rows):
+    if lax.axis_size("tp") != 2:
+        return lax.all_gather(rows, "tp", axis=0, tiled=True)
+    arrived = lax.ppermute(rows, "tp", swap)
+    first = lax.axis_index("tp") == 0
+    return jnp.concatenate(
+        [jnp.where(first, rows, arrived), jnp.where(first, arrived, rows)], axis=0
+    )
+
+
+def tp_scatter(rows):
+    if lax.axis_size("tp") != 2:
+        return lax.psum_scatter(rows, "tp", scatter_dimension=0, tiled=True).astype(jnp.float32)
+    half = rows.shape[0] // 2
+    own = lax.axis_index("tp") * half
+    arrived = lax.ppermute(lax.dynamic_slice_in_dim(rows, half - own, half), "tp", swap)
+    kept = lax.dynamic_slice_in_dim(rows, own, half)
+    return kept.astype(jnp.float32) + arrived.astype(jnp.float32)
+
+
+def sum_all(values):
+    sizes = [value.size for value in values]
+    packed = jnp.concatenate([value.reshape(-1) for value in values])
+    packed = jnp.pad(packed, (0, -packed.size % 1024)).reshape(-1, 128)
+    for axis in ("tp", "fsdp"):
+        count = lax.axis_size(axis)
+        for bit in range(count.bit_length() - 1):
+            pairs = [(device, device ^ (1 << bit)) for device in range(count)]
+            packed = packed + lax.ppermute(packed, axis, pairs)
+    packed = packed.reshape(-1)
+    results, start = [], 0
+    for value, size in zip(values, sizes):
+        results.append(packed[start : start + size].reshape(value.shape))
+        start += size
+    return results
 
 
 def per_device(
@@ -338,7 +378,7 @@
     gain_one = gain_attn.astype(jnp.float32)
     gain_two = gain_moe.astype(jnp.float32)
     hat_attn, factor_attn, normed_attn = norm_rows(token_f, gain_one)
-    attn_in = lax.all_gather(normed_attn, "tp", axis=0, tiled=True)
+    attn_in = tp_gather(normed_attn)
     qkv = jnp.dot(attn_in, qkv_full, preferred_element_type=jnp.float32).astype(jnp.bfloat16)
     table_local = lax.dynamic_slice_in_dim(rel_table, tp_index * heads_local, heads_local, 1)
     place_onehot = (
@@ -353,13 +393,10 @@
     context_flat, attn_probs = attn_forward(
         jnp.reshape(length, (1,)).astype(jnp.int32), qkv, offset_table
     )
-    attn_sum = lax.psum_scatter(
+    attn_sum = tp_scatter(
         lax.dot_general(
             context_flat, out_full, (((1,), (1,)), ((), ())), preferred_element_type=jnp.float32
-        ),
-        "tp",
-        scatter_dimension=0,
-        tiled=True,
+        )
     )
     mid = token_f + attn_sum * local_valid
     hat_moe, factor_moe, normed_moe = norm_rows(mid, gain_two)
@@ -374,9 +411,7 @@
     fraction = counts_all / total_tokens
     grad_out = cotangent.astype(jnp.float32)
     scaled_grad = (grad_out * gate * local_valid).astype(jnp.bfloat16)
-    moe_rows = lax.all_gather(
-        jnp.concatenate([normed_moe, scaled_grad], axis=1), "tp", axis=0, tiled=True
-    )
+    moe_rows = tp_gather(jnp.concatenate([normed_moe, scaled_grad], axis=1))
     slot_ids = jnp.sum(chosen * (jnp.cumsum(chosen, axis=0) - 1), axis=1)
     flat_index = jnp.where(key_valid, routes_group * capacity + slot_ids, slot_count)
     owner = jnp.zeros((slot_count + 1,), jnp.int32).at[flat_index].set(all_pos)[:slot_count]
@@ -396,9 +431,7 @@
         [expert_part.reshape(slot_count, model_width), jnp.zeros((1, model_width), jnp.float32)],
         axis=0,
     )
-    combined = lax.psum_scatter(
-        padded_part[flat_index].astype(jnp.bfloat16), "tp", scatter_dimension=0, tiled=True
-    ).astype(jnp.float32)
+    combined = tp_scatter(padded_part[flat_index].astype(jnp.bfloat16))
     mixed = (mid + gate * combined * local_valid).astype(jnp.bfloat16)
     grad_gate = jnp.sum(grad_out * combined * local_valid, axis=1, keepdims=True)
     order = send_order(shard_rows)
@@ -425,9 +458,7 @@
         [grad_dispatch.reshape(slot_count, model_width), jnp.zeros((1, model_width), jnp.float32)],
         axis=0,
     )
-    grad_normed = lax.psum_scatter(
-        padded_dispatch[flat_index], "tp", scatter_dimension=0, tiled=True
-    )
+    grad_normed = tp_scatter(padded_dispatch[flat_index])
     aux_grad = balance_weight * EXP * fraction / total_tokens
     grad_probs = onehot_local * grad_gate + local_valid * aux_grad[None, :]
     grad_logits = router_probs * (
@@ -440,7 +471,7 @@
     grad_mid_norm, grad_gain_moe = norm_back(grad_normed, hat_moe, factor_moe, gain_two)
     grad_mid = grad_out + grad_mid_norm
     grad_branch = (grad_mid * local_valid).astype(jnp.bfloat16)
-    grad_branch_all = lax.all_gather(grad_branch, "tp", axis=0, tiled=True)
+    grad_branch_all = tp_gather(grad_branch)
     in_rows, down_rows, grad_branch_all = lax.optimization_barrier(
         (in_rows, down_rows, grad_branch_all)
     )
@@ -459,9 +490,7 @@
         == jnp.arange(BUCKETS, dtype=jnp.int32)[None, :]
     ).astype(jnp.float32)
     grad_table_local = jnp.einsum("hm,mb->hb", diag, back_onehot, precision=highest)
-    grad_attn_in = lax.psum_scatter(
-        grad_attn_part.astype(jnp.bfloat16), "tp", scatter_dimension=0, tiled=True
-    ).astype(jnp.float32)
+    grad_attn_in = tp_scatter(grad_attn_part.astype(jnp.bfloat16))
     grad_token_norm, grad_gain_attn = norm_back(grad_attn_in, hat_attn, factor_attn, gain_one)
     grad_tokens = (grad_mid + grad_token_norm).astype(jnp.bfloat16)
     table_full = lax.dynamic_update_slice(
@@ -480,8 +509,8 @@
     grad_out_shard = small_sum[:, 3 * head_width :]
     grad_in_part = in_sum.reshape(shard_rows, EXP, hidden_local)
     grad_down_part = down_sum.reshape(shard_rows, EXP, hidden_local)
-    gain_attn_sum, gain_moe_sum, router_sum, table_sum, prob_all = lax.psum(
-        (grad_gain_attn, grad_gain_moe, grad_router, table_full, prob_local), ("fsdp", "tp")
+    gain_attn_sum, gain_moe_sum, router_sum, table_sum, prob_all = sum_all(
+        (grad_gain_attn, grad_gain_moe, grad_router, table_full, prob_local)
     )
     balance = EXP * jnp.sum(fraction * (prob_all / total_tokens))
     return (

time: 671 us -> 616 us (0.918)
  blocking collectives: 86.2 us -> 0 us
  waiting for transfers between devices: 297 us -> 339 us
  starting transfers between devices: 14.7 us -> 30 us
  local copies, waits for them, and re-layouts: 88.7 us -> 75.3 us
    ppermute x0 -> x12, waiting for transfers between devices: none -> 90 us  [the longest x4 45.9 us: tp_scatter(): lax.ppermute(lax.dynamic_slice_in_dim(rows, half - own, half), 'tp', swap)]
    psum x1 -> x0, blocking collectives: 62 us -> none  [per_device(): lax.psum((grad_gain_attn, grad_gain_moe, grad_router, table_full, prob_lo...]
    all_gather x3, waiting for transfers between devices: 173 us -> 113 us  [gather_rows(): return lax.all_gather(shard, 'fsdp', axis=0, tiled=True)]
    ppermute x20, waiting for transfers between devices: 81.9 us -> 136 us  [halve_rows(): arrived = lax.ppermute(rows[half:], 'fsdp', pairs)]
    reduce_scatter x4 -> x0, waiting for transfers between devices: 24.2 us -> none  [the longest x1 24.2 us: per_device(): lax.psum_scatter(lax.dot_general(context_flat, out_full, (((1,), (1,)), (...]
    all_gather x2 -> x0, blocking collectives: 24.2 us -> none  [the longest x1 12.8 us: per_device(): attn_in = lax.all_gather(normed_attn, 'tp', axis=0, tiled=True)]
    all_gather x1 -> x0, waiting for transfers between devices: 17.7 us -> none  [per_device(): lax.all_gather(jnp.concatenate([normed_moe, scaled_grad], axis=1), 'tp',...]
    ppermute x0 -> x12, starting transfers between devices: none -> 16.6 us  [the longest x3 6.2 us: tp_gather(): arrived = lax.ppermute(rows, 'tp', swap)]
  transfers between devices with their start and end apart: 28 -> 35, of which waited for: 13 -> 22; matrix products, arithmetic and copies ran while one was open for 23% -> 21% of each run, Pallas kernels for 1% -> 3%
where the time goes in v3:
time: 616 us; the launch traced here: 609 us
  waiting for transfers between devices  339 us (55%)
  local copies, waits for them, and re-layouts  75.3 us (12%)
  matrix products  63.2 us (10%)
  other arithmetic  56.2 us (9%)
  starting transfers between devices  30 us (5%)
  Pallas kernels  27 us (4%)
  between operations  18 us (3%)
    ppermute x20, waiting for transfers between devices, halve_rows(): arrived = lax.ppermute(rows[half:], 'fsdp', pairs)  136 us
    all_gather x3, waiting for transfers between devices, gather_rows(): return lax.all_gather(shard, 'fsdp', axis=0, tiled=True)  113 us
    ppermute x4, waiting for transfers between devices, tp_scatter(): lax.ppermute(lax.dynamic_slice_in_dim(rows, half - own, half), 'tp', swap)  45.9 us
    convert_element_type x15, other arithmetic, halve_rows(): return total if step == len(masks) - 1 else total.astype(jnp.bfloat16)  28.2 us
    ppermute x5, waiting for transfers between devices, sum_all(): packed = packed + lax.ppermute(packed, axis, pairs)  23 us
    ppermute x3, waiting for transfers between devices, tp_gather(): arrived = lax.ppermute(rows, 'tp', swap)  21 us
    unnamed x174, local copies, waits for them, and re-layouts  17.8 us
    dot_general x1, matrix products, per_device(): jnp.einsum('ecd,def->ecf', grad_expert, down_full, preferred_element_type...  15.8 us
  transfers between devices with their start and end apart: 35, of which 22 were waited for; matrix products, arithmetic and copies ran while one was open for 21% of the time, Pallas kernels for 3%

profile of v3, /device:TPU:0, one launch (start us, length us, event | category | flops | bytes accessed | tf_op | source)
XLA Modules:
  0.0 609.0 jit_solution(5717623990380887102)
XLA Ops:
  22.9 8.1 %collective-permute-done = bf16[256,768]{1,0:T(8,128)(2,1)S(1)} collective-permute-done((bf16[256,768]{1,0:T(8,128)(2,1)S(1)}, bf16[256,768]{1,0:T(8,128)(2,1)S(1)}, u32[]{:S(2)}, u32[]{:S(2)}) %collective-permute-start) | collective-permute-done | bytes 393248 | tf_op jit(solution)/shard_map/ppermute | solution.py:291
  31.4 30.0 %all-gather.4.cloned.1.call-done = bf16[768,1664]{1,0:T(8,128)(2,1)} async-done(((bf16[48,1664]{1,0:T(8,128)(2,1)}), bf16[768,1664]{1,0:T(8,128)(2,1)}) %all-gather.4.cloned.1.call-update) | async-done | bytes 2555920 | tf_op jit(solution)/shard_map/all_gather | solution.py:241
  64.1 8.5 %attn_forward.1 = (bf16[512,384]{1,0:T(8,128)(2,1)S(1)}, f32[6,512,512]{2,1,0:T(8,128)S(1)}) custom-call(s32[1]{0:T(128)} %dynamic_slice.34.len_ref, bf16[512,1152]{1,0:T(8,128)(2,1)S(1)} %convolution_convert_fusion.1.query_ref.key_ref.value_ref, bf16[512,1152]{1,0:T(8,128)(2,1)S(1)} %convolution_convert_fusion.1.query_ref.key_ref.value_ref, ...), custom_call_target="tpu_custom_call" | custom-call | flops 402653184 | bytes 6291456 | tf_op jit(solution)/shard_map/attn_forward/pallas_call | solution.py:87
  81.8 16.9 %collective-permute-done.1 = f32[256,768]{1,0:T(8,128)} collective-permute-done((f32[256,768]{1,0:T(8,128)S(1)}, f32[256,768]{1,0:T(8,128)}, u32[]{:S(2)}, u32[]{:S(2)}) %collective-permute-start.1) | collective-permute-done | bytes 786464 | tf_op jit(solution)/shard_map/ppermute | solution.py:303
  110.1 12.2 %collective-permute-done.2 = bf16[256,1536]{1,0:T(8,128)(2,1)} collective-permute-done((bf16[256,1536]{1,0:T(8,128)(2,1)S(1)}, bf16[256,1536]{1,0:T(8,128)(2,1)}, u32[]{:S(2)}, u32[]{:S(2)}) %collective-permute-start.2) | collective-permute-done | bytes 786464 | tf_op jit(solution)/shard_map/ppermute | solution.py:291
  132.9 11.0 %all-gather.6.cloned.1.call-done = bf16[768,4,1536]{2,0,1:T(8,128)(2,1)} async-done(((bf16[48,4,1536]{2,0,1:T(8,128)(2,1)}), bf16[768,4,1536]{2,0,1:T(8,128)(2,1)}) %all-gather.6.cloned.1.call-update) | async-done | bytes 9437200 | tf_op jit(solution)/shard_map/all_gather | solution.py:241
  143.9 10.1 %fusion.31 = (u8[192,1536]{1,0:T(8,128)(4,1)}, u8[192,1536]{1,0:T(8,128)(4,1)}, f32[4,192,1536]{2,1,0:T(8,128)}) fusion(bf16[4,192,768]{2,1,0:T(8,128)(2,1)S(1)} %bitcast.77, bf16[768,4,1536]{2,0,1:T(8,128)(2,1)} %all-gather.6.cloned.1.call-done), kind=kOutput, calls=%fused_computation.81 | convolution fusion | flops 1826684928 | bytes 15925248 | tf_op jit(solution)/shard_map/ecd,def->ecf/dot_general | solution.py:427
  154.0 71.9 %all-gather.8.cloned.1.call-done = bf16[768,4,1536]{2,0,1:T(8,128)(2,1)} async-done(((bf16[48,4,1536]{2,0,1:T(8,128)(2,1)}), bf16[768,4,1536]{2,0,1:T(8,128)(2,1)}) %all-gather.8.cloned.1.call-update) | async-done | bytes 9437200 | tf_op jit(solution)/shard_map/all_gather | solution.py:241
  225.9 15.8 %add_convert_fusion.4 = (bf16[4,192,1536]{2,1,0:T(8,128)(2,1)S(1)}, f32[4,192,1536]{2,1,0:T(8,128)S(1)}) fusion(f32[4,192,1536]{2,1,0:T(8,128)} %get-tuple-element.97, u8[192,1536]{1,0:T(8,128)(4,1)} %get-tuple-element.66, u8[192,1536]{1,0:T(8,128)(4,1)} %get-tuple-element.65, bf16[4,192,768]{2,1,0:T(8,128)(2,1)} %bitcast.76, ...), kind=kOutput, calls=%fused_computation.17 | convolution fusion | flops 1902772224 | bytes 23003136 | tf_op jit(solution)/shard_map/ecd,def->ecf/dot_general | solution.py:443
  257.6 6.9 %fusion.101 = bf16[4,192,768]{2,1,0:T(8,128)(2,1)S(1)} fusion(bf16[4,192,1536]{2,1,0:T(8,128)(2,1)S(1)} %multiply_convert_fusion, bf16[768,4,1536]{2,0,1:T(8,128)(2,1)} %all-gather.8.cloned.1.call-done), kind=kOutput, calls=%fused_computation.236 | convolution fusion | flops 1811939328 | bytes 12976128 | tf_op jit(solution)/shard_map/ecf,def->ecd/dot_general | solution.py:429
  265.6 4.6 gather_fusion.1
  278.7 5.6 add_convert_fusion.3
  288.3 6.9 %fusion.102 = f32[4,192,768]{2,1,0:T(8,128)S(1)} fusion(bf16[4,192,1536]{2,1,0:T(8,128)(2,1)S(1)} %get-tuple-element.32, bf16[768,4,1536]{2,0,1:T(8,128)(2,1)} %all-gather.6.cloned.1.call-done), kind=kOutput, calls=%fused_computation.237 | convolution fusion | flops 1811939328 | bytes 14155776 | tf_op jit(solution)/shard_map/ecf,def->ecd/dot_general | solution.py:454
  296.8 4.9 gather_fusion.2
  309.0 23.4 %collective-permute-done.3 = bf16[256,768]{1,0:T(8,128)(2,1)} collective-permute-done((bf16[256,768]{1,0:T(8,128)(2,1)}, bf16[256,768]{1,0:T(8,128)(2,1)}, u32[]{:S(2)}, u32[]{:S(2)}) %collective-permute-start.3) | collective-permute-done | bytes 393248 | tf_op jit(solution)/shard_map/ppermute | solution.py:303
  347.0 4.7 gather_fusion.3
  355.8 12.5 %collective-permute-done.8 = bf16[192,3072]{1,0:T(8,128)(2,1)} collective-permute-done((bf16[192,3072]{1,0:T(8,128)(2,1)}, bf16[192,3072]{1,0:T(8,128)(2,1)}, u32[]{:S(2)}, u32[]{:S(2)}) %collective-permute-start.8) | collective-permute-done | bytes 1179680 | tf_op jit(solution)/shard_map/ppermute | solution.py:274
  371.0 22.1 %collective-permute-done.9 = bf16[192,3072]{1,0:T(8,128)(2,1)} collective-permute-done((bf16[192,3072]{1,0:T(8,128)(2,1)}, bf16[192,3072]{1,0:T(8,128)(2,1)}, u32[]{:S(2)}, u32[]{:S(2)}) %collective-permute-start.9) | collective-permute-done | bytes 1179680 | tf_op jit(solution)/shard_map/ppermute | solution.py:274
  395.8 4.1 add_convert_fusion.1
  403.1 8.2 %attn_backward.1 = (bf16[512,384]{1,0:T(8,128)(2,1)S(1)}, bf16[512,384]{1,0:T(8,128)(2,1)S(1)}, bf16[512,384]{1,0:T(8,128)(2,1)S(1)}, f32[3,2,1024]{2,1,0:T(2,128)S(1)}) custom-call(bf16[512,1152]{1,0:T(8,128)(2,1)S(1)} %convolution_convert_fusion.1.query_ref.key_ref.value_ref, bf16[512,1152]{1,0:T(8,128)(2,1)S(1)} %convolution_convert_fusion.1.query_ref.key_ref.value_ref, ...), custom_call_target="tpu_custom_call" | custom-call | flops 1207959552 | bytes 6291456 | tf_op jit(solution)/shard_map/attn_backward/pallas_call | solution.py:178
  419.7 5.7 collective-permute-done.12
  428.6 4.9 convolution_convert_fusion
  448.6 11.8 %collective-permute-done.16 = f32[40,128]{1,0:T(8,128)S(1)} collective-permute-done((f32[40,128]{1,0:T(8,128)S(1)}, f32[40,128]{1,0:T(8,128)S(1)}, u32[]{:S(2)}, u32[]{:S(2)}) %collective-permute-start.16) | collective-permute-done | bytes 20512 | tf_op jit(solution)/shard_map/ppermute | solution.py:316
  464.2 11.1 %collective-permute-done.17 = f32[40,128]{1,0:T(8,128)S(1)} collective-permute-done((f32[40,128]{1,0:T(8,128)S(1)}, f32[40,128]{1,0:T(8,128)S(1)}, u32[]{:S(2)}, u32[]{:S(2)}) %collective-permute-start.17) | collective-permute-done | bytes 20512 | tf_op jit(solution)/shard_map/ppermute | solution.py:316
  482.7 19.7 %collective-permute-done.28 = bf16[96,3072]{1,0:T(8,128)(2,1)S(1)} collective-permute-done((bf16[96,3072]{1,0:T(8,128)(2,1)}, bf16[96,3072]{1,0:T(8,128)(2,1)S(1)}, u32[]{:S(2)}, u32[]{:S(2)}) %collective-permute-start.28) | collective-permute-done | bytes 589856 | tf_op jit(solution)/shard_map/ppermute | solution.py:274
  502.7 8.8 %collective-permute-done.29 = bf16[48,3072]{1,0:T(8,128)(2,1)S(1)} collective-permute-done((bf16[48,3072]{1,0:T(8,128)(2,1)S(1)}, bf16[48,3072]{1,0:T(8,128)(2,1)S(1)}, u32[]{:S(2)}, u32[]{:S(2)}) %collective-permute-start.29) | collective-permute-done | bytes 294944 | tf_op jit(solution)/shard_map/ppermute | solution.py:274
  522.8 7.0 %collective-permute-done.19 = bf16[192,1536]{1,0:T(8,128)(2,1)S(1)} collective-permute-done((bf16[192,1536]{1,0:T(8,128)(2,1)S(1)}, bf16[192,1536]{1,0:T(8,128)(2,1)S(1)}, u32[]{:S(2)}, u32[]{:S(2)}) %collective-permute-start.19) | collective-permute-done | bytes 589856 | tf_op jit(solution)/shard_map/ppermute | solution.py:274
  530.6 34.3 %collective-permute-done.26 = bf16[96,3072]{1,0:T(8,128)(2,1)S(1)} collective-permute-done((bf16[96,3072]{1,0:T(8,128)(2,1)S(1)}, bf16[96,3072]{1,0:T(8,128)(2,1)S(1)}, u32[]{:S(2)}, u32[]{:S(2)}) %collective-permute-start.26) | collective-permute-done | bytes 589856 | tf_op jit(solution)/shard_map/ppermute | solution.py:274
  565.2 12.5 %collective-permute-done.23 = bf16[96,3072]{1,0:T(8,128)(2,1)S(1)} collective-permute-done((bf16[96,3072]{1,0:T(8,128)(2,1)S(1)}, bf16[96,3072]{1,0:T(8,128)(2,1)S(1)}, u32[]{:S(2)}, u32[]{:S(2)}) %collective-permute-start.23) | collective-permute-done | bytes 589856 | tf_op jit(solution)/shard_map/ppermute | solution.py:274
  577.9 5.9 collective-permute-done.20
  584.0 6.1 %collective-permute-done.27 = bf16[48,3072]{1,0:T(8,128)(2,1)S(1)} collective-permute-done((bf16[48,3072]{1,0:T(8,128)(2,1)S(1)}, bf16[48,3072]{1,0:T(8,128)(2,1)S(1)}, u32[]{:S(2)}, u32[]{:S(2)}) %collective-permute-start.27) | collective-permute-done | bytes 294944 | tf_op jit(solution)/shard_map/ppermute | solution.py:274
  590.2 6.2 %collective-permute-done.24 = bf16[48,3072]{1,0:T(8,128)(2,1)S(1)} collective-permute-done((bf16[48,3072]{1,0:T(8,128)(2,1)S(1)}, bf16[48,3072]{1,0:T(8,128)(2,1)S(1)}, u32[]{:S(2)}, u32[]{:S(2)}) %collective-permute-start.24) | collective-permute-done | bytes 294944 | tf_op jit(solution)/shard_map/ppermute | solution.py:274
  (381 shorter events, 168.3 us)
Async XLA Ops:
  7.2 54.1 %all-gather.4.cloned.1.call-start = ((), (), s32[]{:S(2)}) async-start(), calls=%async_computation | async-start | bytes 2715648 | tf_op jit(solution)/shard_map/all_gather | solution.py:241
  15.5 128.4 %all-gather.6.cloned.1.call-start = ((), (), s32[]{:S(2)}) async-start(), calls=%async_computation.1 | async-start | bytes 10027008 | tf_op jit(solution)/shard_map/all_gather | solution.py:241
  17.6 208.4 %all-gather.8.cloned.1.call-start = ((), (), s32[]{:S(2)}) async-start(), calls=%async_computation.2 | async-start | bytes 10027008 | tf_op jit(solution)/shard_map/all_gather | solution.py:241
  18.9 12.1 %collective-permute-start = (bf16[256,768]{1,0:T(8,128)(2,1)S(1)}, bf16[256,768]{1,0:T(8,128)(2,1)S(1)}, u32[]{:S(2)}, u32[]{:S(2)}) collective-permute-start(bf16[256,768]{1,0:T(8,128)(2,1)S(1)} %fusion.32), channel_id=1, source_target_pairs={{0,1},{1,0},{2,3},{3,2},{4,5},{5,4},{6,7},{7,6},{8,9},{9,8},{10,11... | collective-permute-start | bytes 1179656 | tf_op jit(solution)/shard_map/ppermute | solution.py:291
  78.9 19.9 %collective-permute-start.1 = (f32[256,768]{1,0:T(8,128)S(1)}, f32[256,768]{1,0:T(8,128)}, u32[]{:S(2)}, u32[]{:S(2)}) collective-permute-start(f32[256,768]{1,0:T(8,128)S(1)} %constant_dynamic-slice_fusion.4), channel_id=1, source_target_pairs={{0,1},{1,0},{2,3},{3,2},{4,5},{5,4},{6,7},{7,6},{8,9},{9,8},{10,11... | collective-permute-start | bytes 2359304 | tf_op jit(solution)/shard_map/ppermute | solution.py:303
  102.8 19.4 %collective-permute-start.2 = (bf16[256,1536]{1,0:T(8,128)(2,1)S(1)}, bf16[256,1536]{1,0:T(8,128)(2,1)}, u32[]{:S(2)}, u32[]{:S(2)}) collective-permute-start(bf16[256,1536]{1,0:T(8,128)(2,1)S(1)} %pad_maximum_fusion.5), channel_id=1, source_target_pairs={{0,1},{1,0},{2,3},{3,2},{4,5},{5,4},{6,7},{7,6},{8,9},{9,8},{10,11... | collective-permute-start | bytes 2359304 | tf_op jit(solution)/shard_map/ppermute | solution.py:291
  248.4 30.3 %collective-permute-start.4 = (bf16[384,3072]{1,0:T(8,128)(2,1)}, bf16[384,3072]{1,0:T(8,128)(2,1)}, u32[]{:S(2)}, u32[]{:S(2)}) collective-permute-start(bf16[384,3072]{1,0:T(8,128)(2,1)} %slice.248), channel_id=1, source_target_pairs={{0,2},{2,0},{4,6},{6,4},{8,10},{10,8},{12,14},{14,12},{16,18},{18,... | collective-permute-start | bytes 7077896 | tf_op jit(solution)/shard_map/ppermute | solution.py:274
  254.6 29.8 %collective-permute-start.5 = (bf16[384,3072]{1,0:T(8,128)(2,1)}, bf16[384,3072]{1,0:T(8,128)(2,1)}, u32[]{:S(2)}, u32[]{:S(2)}) collective-permute-start(bf16[384,3072]{1,0:T(8,128)(2,1)} %slice.250), channel_id=1, source_target_pairs={{0,2},{2,0},{4,6},{6,4},{8,10},{10,8},{12,14},{14,12},{16,18},{18,... | collective-permute-start | bytes 7077896 | tf_op jit(solution)/shard_map/ppermute | solution.py:274
  303.9 35.8 %collective-permute-start.10 = (f32[256,768]{1,0:T(8,128)}, f32[256,768]{1,0:T(8,128)}, u32[]{:S(2)}, u32[]{:S(2)}) collective-permute-start(f32[256,768]{1,0:T(8,128)} %constant_dynamic-slice_fusion.1), channel_id=1, source_target_pairs={{0,1},{1,0},{2,3},{3,2},{4,5},{5,4},{6,7},{7,6},{8,9},{9,8},{10,11... | collective-permute-start | bytes 2359304 | tf_op jit(solution)/shard_map/ppermute | solution.py:303
  306.2 26.2 %collective-permute-start.3 = (bf16[256,768]{1,0:T(8,128)(2,1)}, bf16[256,768]{1,0:T(8,128)(2,1)}, u32[]{:S(2)}, u32[]{:S(2)}) collective-permute-start(bf16[256,768]{1,0:T(8,128)(2,1)} %constant_dynamic-slice_fusion.2), channel_id=1, source_target_pairs={{0,1},{1,0},{2,3},{3,2},{4,5},{5,4},{6,7},{7,6},{8,9},{9,8},{10,11... | collective-permute-start | bytes 1179656 | tf_op jit(solution)/shard_map/ppermute | solution.py:303
  338.1 57.7 %collective-permute-start.6 = (bf16[384,3072]{1,0:T(8,128)(2,1)}, bf16[384,3072]{1,0:T(8,128)(2,1)}, u32[]{:S(2)}, u32[]{:S(2)}) collective-permute-start(bf16[384,3072]{1,0:T(8,128)(2,1)} %slice.190), channel_id=1, source_target_pairs={{0,2},{2,0},{4,6},{6,4},{8,10},{10,8},{12,14},{14,12},{16,18},{18,... | collective-permute-start | bytes 7077896 | tf_op jit(solution)/shard_map/ppermute | solution.py:274
  339.2 29.1 %collective-permute-start.8 = (bf16[192,3072]{1,0:T(8,128)(2,1)}, bf16[192,3072]{1,0:T(8,128)(2,1)}, u32[]{:S(2)}, u32[]{:S(2)}) collective-permute-start(bf16[192,3072]{1,0:T(8,128)(2,1)} %slice.194), channel_id=1, source_target_pairs={{0,4},{2,6},{4,0},{6,2},{8,12},{10,14},{12,8},{14,10},{16,20},{18,... | collective-permute-start | bytes 3538952 | tf_op jit(solution)/shard_map/ppermute | solution.py:274
  343.1 11.4 %collective-permute-start.11 = (bf16[256,768]{1,0:T(8,128)(2,1)}, bf16[256,768]{1,0:T(8,128)(2,1)}, u32[]{:S(2)}, u32[]{:S(2)}) collective-permute-start(bf16[256,768]{1,0:T(8,128)(2,1)} %multiply_convert_fusion.1), channel_id=1, source_target_pairs={{0,1},{1,0},{2,3},{3,2},{4,5},{5,4},{6,7},{7,6},{8,9},{9,8},{10,11... | collective-permute-start | bytes 1179656 | tf_op jit(solution)/shard_map/ppermute | solution.py:291
  345.7 47.5 %collective-permute-start.9 = (bf16[192,3072]{1,0:T(8,128)(2,1)}, bf16[192,3072]{1,0:T(8,128)(2,1)}, u32[]{:S(2)}, u32[]{:S(2)}) collective-permute-start(bf16[192,3072]{1,0:T(8,128)(2,1)} %slice.196), channel_id=1, source_target_pairs={{0,4},{2,6},{4,0},{6,2},{8,12},{10,14},{12,8},{14,10},{16,20},{18,... | collective-permute-start | bytes 3538952 | tf_op jit(solution)/shard_map/ppermute | solution.py:274
  353.7 46.2 %collective-permute-start.7 = (bf16[384,3072]{1,0:T(8,128)(2,1)S(1)}, bf16[384,3072]{1,0:T(8,128)(2,1)S(1)}, u32[]{:S(2)}, u32[]{:S(2)}) collective-permute-start(bf16[384,3072]{1,0:T(8,128)(2,1)S(1)} %slice.192), channel_id=1, source_target_pairs={{0,2},{2,0},{4,6},{6,4},{8,10},{10,8},{12,14},{14,12},{16,18},{18,... | collective-permute-start | bytes 7077896 | tf_op jit(solution)/shard_map/ppermute | solution.py:274
  414.5 10.9 %collective-permute-start.12 = (bf16[256,768]{1,0:T(8,128)(2,1)}, bf16[256,768]{1,0:T(8,128)(2,1)S(1)}, u32[]{:S(2)}, u32[]{:S(2)}) collective-permute-start(bf16[256,768]{1,0:T(8,128)(2,1)} %constant_dynamic-slice_fusion), channel_id=1, source_target_pairs={{0,1},{1,0},{2,3},{3,2},{4,5},{5,4},{6,7},{7,6},{8,9},{9,8},{10,11... | collective-permute-start | bytes 1179656 | tf_op jit(solution)/shard_map/ppermute | solution.py:303
  437.1 10.9 %collective-permute-start.15 = (f32[40,128]{1,0:T(8,128)S(1)}, f32[40,128]{1,0:T(8,128)S(1)}, u32[]{:S(2)}, u32[]{:S(2)}) collective-permute-start(f32[40,128]{1,0:T(8,128)S(1)} %fusion.122), channel_id=1, source_target_pairs={{0,4},{2,6},{4,0},{6,2},{8,12},{10,14},{12,8},{14,10},{16,20},{18,... | collective-permute-start | bytes 61448 | tf_op jit(solution)/shard_map/ppermute | solution.py:316
  440.4 73.1 %collective-permute-start.18 = (bf16[384,1536]{1,0:T(8,128)(2,1)}, bf16[384,1536]{1,0:T(8,128)(2,1)}, u32[]{:S(2)}, u32[]{:S(2)}) collective-permute-start(bf16[384,1536]{1,0:T(8,128)(2,1)} %pad_maximum_fusion.1), channel_id=1, source_target_pairs={{0,2},{2,0},{4,6},{6,4},{8,10},{10,8},{12,14},{14,12},{16,18},{18,... | collective-permute-start | bytes 3538952 | tf_op jit(solution)/shard_map/ppermute | solution.py:274
  441.6 74.8 %collective-permute-start.25 = (bf16[192,3072]{1,0:T(8,128)(2,1)}, bf16[192,3072]{1,0:T(8,128)(2,1)}, u32[]{:S(2)}, u32[]{:S(2)}) collective-permute-start(bf16[192,3072]{1,0:T(8,128)(2,1)} %slice.221), channel_id=1, source_target_pairs={{0,4},{2,6},{4,0},{6,2},{8,12},{10,14},{12,8},{14,10},{16,20},{18,... | collective-permute-start | bytes 3538952 | tf_op jit(solution)/shard_map/ppermute | solution.py:274
  444.2 74.8 %collective-permute-start.22 = (bf16[192,3072]{1,0:T(8,128)(2,1)}, bf16[192,3072]{1,0:T(8,128)(2,1)}, u32[]{:S(2)}, u32[]{:S(2)}) collective-permute-start(bf16[192,3072]{1,0:T(8,128)(2,1)} %slice.215), channel_id=1, source_target_pairs={{0,4},{2,6},{4,0},{6,2},{8,12},{10,14},{12,8},{14,10},{16,20},{18,... | collective-permute-start | bytes 3538952 | tf_op jit(solution)/shard_map/ppermute | solution.py:274
  445.6 33.6 %collective-permute-start.30 = (bf16[96,3072]{1,0:T(8,128)(2,1)}, bf16[96,3072]{1,0:T(8,128)(2,1)}, u32[]{:S(2)}, u32[]{:S(2)}) collective-permute-start(bf16[96,3072]{1,0:T(8,128)(2,1)} %slice.231), channel_id=1, source_target_pairs={{0,16},{2,18},{4,20},{6,22},{8,24},{10,26},{12,28},{14,30},{16,0},... | collective-permute-start | bytes 1769480 | tf_op jit(solution)/shard_map/ppermute | solution.py:274
  448.0 12.5 %collective-permute-start.16 = (f32[40,128]{1,0:T(8,128)S(1)}, f32[40,128]{1,0:T(8,128)S(1)}, u32[]{:S(2)}, u32[]{:S(2)}) collective-permute-start(f32[40,128]{1,0:T(8,128)S(1)} %add.403), channel_id=1, source_target_pairs={{0,8},{2,10},{4,12},{6,14},{8,0},{10,2},{12,4},{14,6},{16,24},{18,... | collective-permute-start | bytes 61448 | tf_op jit(solution)/shard_map/ppermute | solution.py:316
  460.4 15.0 %collective-permute-start.17 = (f32[40,128]{1,0:T(8,128)S(1)}, f32[40,128]{1,0:T(8,128)S(1)}, u32[]{:S(2)}, u32[]{:S(2)}) collective-permute-start(f32[40,128]{1,0:T(8,128)S(1)} %add.404), channel_id=1, source_target_pairs={{0,16},{2,18},{4,20},{6,22},{8,24},{10,26},{12,28},{14,30},{16,0},... | collective-permute-start | bytes 61448 | tf_op jit(solution)/shard_map/ppermute | solution.py:316
  475.4 27.0 %collective-permute-start.28 = (bf16[96,3072]{1,0:T(8,128)(2,1)}, bf16[96,3072]{1,0:T(8,128)(2,1)S(1)}, u32[]{:S(2)}, u32[]{:S(2)}) collective-permute-start(bf16[96,3072]{1,0:T(8,128)(2,1)} %slice.227), channel_id=1, source_target_pairs={{0,16},{2,18},{4,20},{6,22},{8,24},{10,26},{12,28},{14,30},{16,0},... | collective-permute-start | bytes 1769480 | tf_op jit(solution)/shard_map/ppermute | solution.py:274
  480.6 22.0 %collective-permute-start.31 = (bf16[48,3072]{1,0:T(8,128)(2,1)S(1)}, bf16[48,3072]{1,0:T(8,128)(2,1)S(1)}, u32[]{:S(2)}, u32[]{:S(2)}) collective-permute-start(bf16[48,3072]{1,0:T(8,128)(2,1)S(1)} %slice.277), channel_id=1, source_target_pairs={{0,8},{2,10},{4,12},{6,14},{8,0},{10,2},{12,4},{14,6},{16,24},{18,... | collective-permute-start | bytes 884744 | tf_op jit(solution)/shard_map/ppermute | solution.py:274
  515.3 14.5 %collective-permute-start.19 = (bf16[192,1536]{1,0:T(8,128)(2,1)S(1)}, bf16[192,1536]{1,0:T(8,128)(2,1)S(1)}, u32[]{:S(2)}, u32[]{:S(2)}) collective-permute-start(bf16[192,1536]{1,0:T(8,128)(2,1)S(1)} %slice.257), channel_id=1, source_target_pairs={{0,4},{2,6},{4,0},{6,2},{8,12},{10,14},{12,8},{14,10},{16,20},{18,... | collective-permute-start | bytes 1769480 | tf_op jit(solution)/shard_map/ppermute | solution.py:274
  518.1 46.8 %collective-permute-start.26 = (bf16[96,3072]{1,0:T(8,128)(2,1)S(1)}, bf16[96,3072]{1,0:T(8,128)(2,1)S(1)}, u32[]{:S(2)}, u32[]{:S(2)}) collective-permute-start(bf16[96,3072]{1,0:T(8,128)(2,1)S(1)} %slice.271), channel_id=1, source_target_pairs={{0,16},{2,18},{4,20},{6,22},{8,24},{10,26},{12,28},{14,30},{16,0},... | collective-permute-start | bytes 1769480 | tf_op jit(solution)/shard_map/ppermute | solution.py:274
  520.6 57.1 %collective-permute-start.23 = (bf16[96,3072]{1,0:T(8,128)(2,1)S(1)}, bf16[96,3072]{1,0:T(8,128)(2,1)S(1)}, u32[]{:S(2)}, u32[]{:S(2)}) collective-permute-start(bf16[96,3072]{1,0:T(8,128)(2,1)S(1)} %slice.267), channel_id=1, source_target_pairs={{0,16},{2,18},{4,20},{6,22},{8,24},{10,26},{12,28},{14,30},{16,0},... | collective-permute-start | bytes 1769480 | tf_op jit(solution)/shard_map/ppermute | solution.py:274
  530.0 53.9 %collective-permute-start.20 = (bf16[96,1536]{1,0:T(8,128)(2,1)S(1)}, bf16[96,1536]{1,0:T(8,128)(2,1)S(1)}, u32[]{:S(2)}, u32[]{:S(2)}) collective-permute-start(bf16[96,1536]{1,0:T(8,128)(2,1)S(1)} %slice.259), channel_id=1, source_target_pairs={{0,16},{2,18},{4,20},{6,22},{8,24},{10,26},{12,28},{14,30},{16,0},... | collective-permute-start | bytes 884744 | tf_op jit(solution)/shard_map/ppermute | solution.py:274
  565.1 25.0 %collective-permute-start.27 = (bf16[48,3072]{1,0:T(8,128)(2,1)S(1)}, bf16[48,3072]{1,0:T(8,128)(2,1)S(1)}, u32[]{:S(2)}, u32[]{:S(2)}) collective-permute-start(bf16[48,3072]{1,0:T(8,128)(2,1)S(1)} %slice.273), channel_id=1, source_target_pairs={{0,8},{2,10},{4,12},{6,14},{8,0},{10,2},{12,4},{14,6},{16,24},{18,... | collective-permute-start | bytes 884744 | tf_op jit(solution)/shard_map/ppermute | solution.py:274
  577.9 18.6 %collective-permute-start.24 = (bf16[48,3072]{1,0:T(8,128)(2,1)S(1)}, bf16[48,3072]{1,0:T(8,128)(2,1)S(1)}, u32[]{:S(2)}, u32[]{:S(2)}) collective-permute-start(bf16[48,3072]{1,0:T(8,128)(2,1)S(1)} %slice.269), channel_id=1, source_target_pairs={{0,8},{2,10},{4,12},{6,14},{8,0},{10,2},{12,4},{14,6},{16,24},{18,... | collective-permute-start | bytes 884744 | tf_op jit(solution)/shard_map/ppermute | solution.py:274
  583.9 15.6 %collective-permute-start.21 = (bf16[48,1536]{1,0:T(8,128)(2,1)S(1)}, bf16[48,1536]{1,0:T(8,128)(2,1)S(1)}, u32[]{:S(2)}, u32[]{:S(2)}) collective-permute-start(bf16[48,1536]{1,0:T(8,128)(2,1)S(1)} %slice.261), channel_id=1, source_target_pairs={{0,8},{2,10},{4,12},{6,14},{8,0},{10,2},{12,4},{14,6},{16,24},{18,... | collective-permute-start | bytes 442376 | tf_op jit(solution)/shard_map/ppermute | solution.py:274
  (85 other events, 1175.3 us)
Sparse Core Ops, SparseCore 0:
  15.6 45.6 all-gather.3
  63.7 80.2 all-gather.5
  146.2 79.6 all-gather.7
